TPU v7x, 256 devices: a whole 4x4x8 slice. The times are simulated.
256 devices in a mesh: dp: 8 (over x, z_lo), tensor: 32 (over y, z_hi, core).
Axes of the slice: x: 4, y: 4, z: 8 (z_hi: 4, z_lo: 2; z = z_hi * 2 + z_lo), core: 2. Of those that a mesh axis runs over, the one named last changes fastest.
Arguments:
- normed: bfloat16 [8, 256, 16384], P('dp', None, 'tensor'), may hold values from -24 to 24
- queries: bfloat16 [8, 256, 8192], P('dp', None, 'tensor'), may hold values from -17 to 17
- keys: bfloat16 [8, 256, 512], P('dp', None, 'tensor'), may hold values from -5 to 5
- values: bfloat16 [8, 256, 512], P('dp', None, 'tensor'), may hold values from -5 to 5
- context_grad: bfloat16 [8, 256, 8192], P('dp', None, 'tensor'), may hold values from -5 to 5
- segments: int32 [8, 256], P('dp'), may hold values from 0 to 3, as said below
- w_query: bfloat16 [16384, 8192], P('tensor'), may hold values from -0.046875 to 0.046875
- w_key: bfloat16 [16384, 512], P('tensor'), may hold values from -0.046875 to 0.046875
- w_value: bfloat16 [16384, 512], P('tensor'), may hold values from -0.046875 to 0.046875
- adapter_down: bfloat16 [3, 16, 16384], P(None, None, 'tensor'), may hold values from -0.046875 to 0.046875
- up_query: bfloat16 [16, 8192], P(None, 'tensor'), may hold values from -0.59765625 to 0.59765625
- up_keyvalue: bfloat16 [2, 16, 512], P(None, None, 'tensor'), may hold values from -0.1796875 to 0.1796875
- accum_down: float32 [3, 16, 16384], P(None, 'dp', 'tensor'), may hold values from -1.2 to 1.2
- accum_query: float32 [16, 8192], P('dp', 'tensor'), may hold values from -0.3 to 0.3
- accum_keyvalue: float32 [2, 16, 512], P(None, 'dp', 'tensor'), may hold values from -0.6 to 0.6
Outputs:
- input_grad: bfloat16 [8, 256, 16384], P('dp', None, 'tensor')
- accum_down_new: float32 [3, 16, 16384], P(None, 'dp', 'tensor')
- accum_query_new: float32 [16, 8192], P('dp', 'tensor')
- accum_keyvalue_new: float32 [2, 16, 512], P(None, 'dp', 'tensor')
Inputs may be any that keep to these rules, and one draw needn't show every extreme that they name: `segments`: within each sequence the ids begin at 0, never fall, and the last token's id is 3.
All inputs are finite; a program needn't handle non-finite values.
Results may differ from a plain program's by a relative error of at most 0.0059.
Values may be sent and summed in bfloat16 or wider, within the bound.
A program may use at most 64 MiB of HBM per device.

v0:
```python
import math

import jax
import jax.numpy as jnp
from jax import lax
from jax.sharding import PartitionSpec as P

KVH = 4
HD = 128
RANK = 16


ADAPTER_SCALE = 2.0
ROPE_BASE = 500000.0
HIGH = lax.Precision.HIGHEST


def rotary_tables(length, width):
    exponent = jnp.arange(width // 2, dtype=jnp.float32) * (2.0 / width)
    frequency = 1.0 / ROPE_BASE**exponent
    wavelength = 2.0 * math.pi / frequency
    blend = (8192.0 / wavelength - 1.0) / 3.0
    middle = (1.0 - blend) * frequency / 8.0 + blend * frequency
    scaled = jnp.where(
        wavelength < 2048.0, frequency, jnp.where(wavelength > 8192.0, frequency / 8.0, middle)
    )
    angle = jnp.arange(length, dtype=jnp.float32)[:, None] * scaled[None, :]
    angle = jnp.concatenate([angle, angle], axis=1)
    return (jnp.cos(angle), jnp.sin(angle))


def unrotate(grads, cosine, sine):
    half_width = grads.shape[-1] // 2
    turned = grads * sine[:, None, :]
    flipped = jnp.concatenate([-turned[..., half_width:], turned[..., :half_width]], axis=-1)
    return grads * cosine[:, None, :] - flipped


def contract_last(left, right):
    return lax.dot_general(
        left, right, (((1,), (1,)), ((), ())), preferred_element_type=jnp.float32
    )


def per_device(
    normed,
    queries,
    keys,
    values,
    context_grad,
    segments,
    w_query,
    w_key,
    w_value,
    adapter_down,
    up_query,
    up_keyvalue,
    accum_down,
    accum_query,
    accum_keyvalue,
):
    length = queries.shape[1]
    heads_here = queries.shape[2] // HD
    score_scale = 1.0 / math.sqrt(HD)
    tensor_index = lax.axis_index("tensor")
    kv_width = keys.shape[2]
    normed_rows = normed[0]
    adapter_local = adapter_down.reshape(3 * RANK, normed_rows.shape[1])
    down_part = contract_last(normed_rows, adapter_local)
    down_early = lax.psum(down_part, "tensor")
    key_all, value_all = (
        lax.all_gather(keys[0], "tensor", axis=1, tiled=True),
        lax.all_gather(values[0], "tensor", axis=1, tiled=True),
    )
    first_head = tensor_index * heads_here
    owner_kv = (first_head + jnp.arange(heads_here, dtype=jnp.int32)) % KVH
    selector = owner_kv[:, None] == jnp.arange(KVH, dtype=jnp.int32)[None, :]
    select_half = selector.astype(jnp.bfloat16)
    select_full = selector.astype(jnp.float32)
    key_heads = jnp.einsum(
        "skd,hk->shd",
        key_all.reshape(length, KVH, HD),
        select_half,
        preferred_element_type=jnp.float32,
    ).astype(jnp.bfloat16)
    value_heads = jnp.einsum(
        "skd,hk->shd",
        value_all.reshape(length, KVH, HD),
        select_half,
        preferred_element_type=jnp.float32,
    ).astype(jnp.bfloat16)
    block_rows = min(512, length)
    block_count = length // block_rows
    positions = jnp.arange(length, dtype=jnp.int32)
    doc_ids = segments[0]
    query_blocks = queries[0].reshape(block_count, block_rows, heads_here, HD)
    cot_blocks = context_grad[0].reshape(block_count, block_rows, heads_here, HD)
    place_blocks = positions.reshape(block_count, block_rows)
    doc_blocks = doc_ids.reshape(block_count, block_rows)

    def attend_block(carry, item):
        key_acc, value_acc = carry
        query_rows, cot_rows, place_rows, doc_rows = item
        allowed = (positions[None, :] <= place_rows[:, None]) & (
            doc_ids[None, :] == doc_rows[:, None]
        )
        scores = (
            jnp.einsum("thd,shd->hts", query_rows, key_heads, preferred_element_type=jnp.float32)
            * score_scale
        )
        scores = jnp.where(allowed[None], scores, -jnp.inf)
        weights = jnp.exp(scores - jnp.max(scores, axis=2, keepdims=True))
        weights = weights / jnp.sum(weights, axis=2, keepdims=True)
        weight_grad = jnp.einsum(
            "thd,shd->hts", cot_rows, value_heads, preferred_element_type=jnp.float32
        )
        row_delta = jnp.sum(weights * weight_grad, axis=2, keepdims=True)
        score_grad = (weights * (weight_grad - row_delta)).astype(jnp.bfloat16)
        weight_half = weights.astype(jnp.bfloat16)
        query_rot = (
            jnp.einsum("hts,shd->thd", score_grad, key_heads, preferred_element_type=jnp.float32)
            * score_scale
        )
        key_acc = (
            key_acc
            + jnp.einsum("hts,thd->shd", score_grad, query_rows, preferred_element_type=jnp.float32)
            * score_scale
        )
        value_acc = value_acc + jnp.einsum(
            "hts,thd->shd", weight_half, cot_rows, preferred_element_type=jnp.float32
        )
        return ((key_acc, value_acc), query_rot)

    empty = jnp.zeros((length, heads_here, HD), jnp.float32)
    (key_part, value_part), query_rot = lax.scan(
        attend_block, (empty, empty), (query_blocks, cot_blocks, place_blocks, doc_blocks)
    )
    query_rot = query_rot.reshape(length, heads_here, HD)
    key_part = jnp.einsum("shd,hk->skd", key_part, select_full, precision=HIGH)
    value_part = jnp.einsum("shd,hk->skd", value_part, select_full, precision=HIGH)
    cosine, sine = rotary_tables(length, HD)
    query_grad = (
        unrotate(query_rot, cosine, sine).astype(jnp.bfloat16).reshape(length, heads_here * HD)
    )
    key_flat = unrotate(key_part, cosine, sine).reshape(length, KVH * HD)
    value_flat = value_part.reshape(length, KVH * HD)
    key_sum, value_sum = lax.psum((key_flat, value_flat), "tensor")
    key_grad = key_sum.astype(jnp.bfloat16)
    value_grad = value_sum.astype(jnp.bfloat16)
    key_own = lax.dynamic_slice_in_dim(key_grad, tensor_index * kv_width, kv_width, 1)
    value_own = lax.dynamic_slice_in_dim(value_grad, tensor_index * kv_width, kv_width, 1)
    frozen = contract_last(key_grad, w_key) + contract_last(value_grad, w_value)
    query_all = lax.all_gather(query_grad, "tensor", axis=1, tiled=True)
    frozen = frozen + contract_last(query_all, w_query)
    up_part = ADAPTER_SCALE * jnp.concatenate(
        [
            contract_last(query_grad, up_query),
            contract_last(key_own, up_keyvalue[0]),
            contract_last(value_own, up_keyvalue[1]),
        ],
        axis=1,
    )
    up_sum = lax.psum(up_part, "tensor")
    input_grad = frozen + jnp.dot(
        up_sum.astype(jnp.bfloat16), adapter_local, preferred_element_type=jnp.float32
    )
    input_grad = input_grad.astype(jnp.bfloat16)[None]
    down_half = down_early.astype(jnp.bfloat16)
    grad_down = jnp.dot(up_sum.T, normed_rows.astype(jnp.float32), precision=HIGH).reshape(
        3, RANK, normed_rows.shape[1]
    )
    grad_query = ADAPTER_SCALE * jnp.dot(
        down_half[:, :RANK].T, query_grad, preferred_element_type=jnp.float32
    )
    grad_keyvalue = ADAPTER_SCALE * jnp.stack(
        [
            jnp.dot(down_half[:, RANK : 2 * RANK].T, key_own, preferred_element_type=jnp.float32),
            jnp.dot(down_half[:, 2 * RANK :].T, value_own, preferred_element_type=jnp.float32),
        ]
    )
    sum_down, sum_query, sum_keyvalue = (
        lax.psum_scatter(grad_down, "dp", scatter_dimension=1, tiled=True),
        lax.psum_scatter(grad_query, "dp", scatter_dimension=0, tiled=True),
        lax.psum_scatter(grad_keyvalue, "dp", scatter_dimension=1, tiled=True),
    )
    tokens_all = lax.axis_size("dp") * length
    return (
        input_grad,
        accum_down + sum_down / tokens_all,
        accum_query + sum_query / tokens_all,
        accum_keyvalue + sum_keyvalue / tokens_all,
    )


def solution(mesh):
    in_specs = (
        P("dp", None, "tensor"),
        P("dp", None, "tensor"),
        P("dp", None, "tensor"),
        P("dp", None, "tensor"),
        P("dp", None, "tensor"),
        P("dp", None),
        P("tensor", None),
        P("tensor", None),
        P("tensor", None),
        P(None, None, "tensor"),
        P(None, "tensor"),
        P(None, None, "tensor"),
        P(None, "dp", "tensor"),
        P("dp", "tensor"),
        P(None, "dp", "tensor"),
    )
    out_specs = (
        P("dp", None, "tensor"),
        P(None, "dp", "tensor"),
        P("dp", "tensor"),
        P(None, "dp", "tensor"),
    )
    return jax.shard_map(
        per_device, mesh=mesh, in_specs=in_specs, out_specs=out_specs, check_vma=False
    )
```

profile of v0, /device:TPU:1, one launch (start us, length us, event | category | flops | bytes accessed | tf_op | source)
XLA Modules:
  0.0 485.9 jit_solution(16034063482283780071)
XLA Ops:
  8.1 50.0 %all-gather = bf16[1,256,512]{1,2,0:T(8,128)(2,1)S(1)} all-gather(bf16[1,256,16]{1,2,0:T(8,128)(2,1)} %param.17), channel_id=2, replica_groups=mesh['dp'=8,'tensor'=32] {'tensor'}, dimensions={2}, use_global_device_ids=true | all-gather | bytes 270336 | tf_op jit(solution)/shard_map/all_gather | solution.py:72
  58.7 0.9 squeeze.30
  59.7 0.9 fusion.20
  60.5 40.1 %all-gather.1 = bf16[1,256,512]{1,2,0:T(8,128)(2,1)S(1)} all-gather(bf16[1,256,16]{1,2,0:T(8,128)(2,1)} %param.18), channel_id=3, replica_groups=mesh['dp'=8,'tensor'=32] {'tensor'}, dimensions={2}, use_global_device_ids=true | all-gather | bytes 270336 | tf_op jit(solution)/shard_map/all_gather | solution.py:73
  101.2 0.9 squeeze.32
  102.1 0.4 fusion.71
  102.5 0.6 fusion.18
  103.7 0.9 fusion.9
  104.7 0.6 fusion.28
  105.7 0.9 fusion.15
  106.6 0.4 maximum_subtract_fusion
  107.1 144.7 %all-reduce.11 = (bf16[256,512]{1,0:T(8,128)(2,1)S(1)}, bf16[256,512]{1,0:T(8,128)(2,1)S(1)}) all-reduce(f32[256,512]{1,0:T(8,128)S(1)} %get-tuple-element.58, f32[256,512]{1,0:T(8,128)S(1)} %get-tuple-element.57), channel_id=1, replica_groups=mesh['dp'=8,'tensor'=32] {'tensor'}, use_global_device_ids=true, to_apply=%region_3.4 | all-reduce | flops 262144 | bytes 1572864 | tf_op jit(solution)/shard_map/psum | solution.py:147
  253.2 138.5 %all-reduce.12 = (f32[256,48]{0,1:T(8,128)S(1)}, bf16[256,48]{0,1:T(8,128)(2,1)S(1)}) all-reduce(f32[256,48]{0,1:T(8,128)S(1)} %maximum_multiply_fusion, f32[256,48]{0,1:T(8,128)S(1)} %fusion.13), channel_id=1, replica_groups=mesh['dp'=8,'tensor'=32] {'tensor'}, use_global_device_ids=true, to_apply=%region_5.6 | all-reduce | flops 24576 | bytes 172032 | tf_op jit(solution)/shard_map/psum | solution.py:163
  391.6 0.9 fusion.11
  392.6 0.5 all-gather.4.cloned.1.call-update
  393.1 0.6 dynamic-slice
  394.8 1.1 convolution_multiply_fusion.2
  395.8 28.1 %all-reduce.5 = (f32[16,256]{1,0:T(8,128)S(1)}, f32[2,16,16]{2,1,0:T(8,128)S(1)}) all-reduce(f32[16,256]{1,0:T(8,128)S(1)} %convolution_multiply_fusion.2, f32[2,16,16]{2,1,0:T(8,128)S(1)} %maximum_multiply_fusion.1), channel_id=5, replica_groups=mesh['dp'=8,'tensor'=32] {'dp'}, use_global_device_ids=true, to_apply=%region_8.9.clone | all-reduce | flops 4608 | bytes 36864
  424.0 0.6 fusion.46
  424.6 0.6 fusion.47
  425.5 43.2 %all-reduce.10.cloned.1.call-done = f32[3,16,512]{2,1,0:T(8,128)} async-done(((f32[3,16,512]{2,1,0:T(8,128)}), f32[3,16,512]{2,1,0:T(8,128)}) %all-reduce.10.cloned.1.call-update) | async-done | bytes 98320
  468.7 1.4 fusion.38
  470.1 7.0 %fusion.75 = f32[256,512]{1,0:T(8,128)S(1)} fusion(bf16[256,8192]{0,1:T(8,128)(2,1)} %all-gather.4.cloned.1.call-done, bf16[512,8192]{1,0:T(8,128)(2,1)} %param.21), kind=kOutput, calls=%fused_computation.103 | convolution fusion | flops 2147483648 | bytes 13107200 | tf_op jit(solution)/shard_map/dot_general | solution.py:40
  477.5 1.0 fusion.7
  (55 shorter events, 4.8 us)
Async XLA Ops:
  8.0 417.2 %copy-start = (bf16[512,512]{1,0:T(8,128)(2,1)S(1)}, bf16[512,512]{1,0:T(8,128)(2,1)}, u32[]{:S(2)}) copy-start(bf16[512,512]{1,0:T(8,128)(2,1)} %param.22) | copy-start | bytes 1572868
  8.0 460.7 %all-reduce.10.cloned.1.call-start = ((), (), s32[]{:S(2)}) async-start(), calls=%async_computation.1 | async-start | bytes 196608
  102.5 149.3 %copy-start.7 = (bf16[2,16,16]{2,1,0:T(8,128)(2,1)S(1)}, bf16[2,16,16]{2,1,0:T(8,128)(2,1)}, u32[]{:S(2)}) copy-start(bf16[2,16,16]{2,1,0:T(8,128)(2,1)} %param.26) | copy-start | bytes 3076
  103.1 149.6 %copy-start.2 = (bf16[1,256,512]{2,1,0:T(8,128)(2,1)S(1)}, bf16[1,256,512]{2,1,0:T(8,128)(2,1)}, u32[]{:S(2)}) copy-start(bf16[1,256,512]{2,1,0:T(8,128)(2,1)} %param.15) | copy-start | bytes 786436
  103.1 149.6 %copy-start.4 = (bf16[3,16,512]{2,1,0:T(8,128)(2,1)S(1)}, bf16[3,16,512]{2,1,0:T(8,128)(2,1)}, u32[]{:S(2)}) copy-start(bf16[3,16,512]{2,1,0:T(8,128)(2,1)} %param.24) | copy-start | bytes 147460
  103.4 149.6 %copy-start.6 = (bf16[16,256]{1,0:T(8,128)(2,1)S(1)}, bf16[16,256]{1,0:T(8,128)(2,1)}, u32[]{:S(2)}) copy-start(bf16[16,256]{1,0:T(8,128)(2,1)} %param.25) | copy-start | bytes 24580
  103.5 289.6 %copy-start.10 = (u32[256]{0:T(256)S(1)}, u32[256]{0:T(256)}, u32[]{:S(2)}) copy-start(u32[256]{0:T(256)} %constant.96) | copy-start | bytes 3076
  103.5 320.5 %copy-start.8 = (f32[2,2,16]{2,1,0:T(2,128)S(1)}, f32[2,2,16]{2,1,0:T(2,128)}, u32[]{:S(2)}) copy-start(f32[2,2,16]{2,1,0:T(2,128)} %param.29) | copy-start | bytes 772
  103.5 321.1 %copy-start.9 = (f32[2,256]{1,0:T(2,128)S(1)}, f32[2,256]{1,0:T(2,128)}, u32[]{:S(2)}) copy-start(f32[2,256]{1,0:T(2,128)} %param.28) | copy-start | bytes 6148
  104.6 364.1 %copy-start.5 = (f32[3,2,512]{2,1,0:T(2,128)S(1)}, f32[3,2,512]{2,1,0:T(2,128)}, u32[]{:S(2)}) copy-start(f32[3,2,512]{2,1,0:T(2,128)} %param.27) | copy-start | bytes 36868
  253.0 139.6 %copy-start.1 = (bf16[256,2,128]{0,2,1:T(8,128)(2,1)}, bf16[256,2,128]{0,2,1:T(8,128)(2,1)S(1)}, u32[]{:S(2)}) copy-start(bf16[256,2,128]{0,2,1:T(8,128)(2,1)S(1)} %fusion.10) | copy-start | bytes 393220
  392.5 77.6 %all-gather.4.cloned.1.call-start = ((), (), s32[]{:S(2)}) async-start(), calls=%async_computation | async-start | bytes 4325376 | tf_op jit(solution)/shard_map/all_gather | solution.py:153
  425.1 52.0 %copy-start.3 = (bf16[512,512]{1,0:T(8,128)(2,1)S(1)}, bf16[512,512]{1,0:T(8,128)(2,1)}, u32[]{:S(2)}) copy-start(bf16[512,512]{1,0:T(8,128)(2,1)} %param.23) | copy-start | bytes 1572868
Sparse Core Ops, SparseCore 0:
  392.6 76.0 all-reduce.9
Sparse Core Ops, SparseCore 1:
  396.1 61.4 all-gather.3
where the time goes:
time: 489 us; the launch traced here: 486 us
  blocking collectives  401 us (82%)
  waiting for transfers between devices  43.8 us (9%)
  between operations  16.5 us (3%)
  matrix products  15.8 us (3%)
  other arithmetic  5.12 us (1%)
    psum x1, blocking collectives, per_device(): key_sum, value_sum = lax.psum((key_flat, value_flat), 'tensor')  145 us
    psum x1, blocking collectives, per_device(): up_sum = lax.psum(up_part, 'tensor')  138 us
    all_gather x1, blocking collectives, per_device(): lax.all_gather(keys[0], 'tensor', axis=1, tiled=True)  50 us
    unnamed x3, waiting for transfers between devices  43.8 us
    all_gather x1, blocking collectives, per_device(): lax.all_gather(values[0], 'tensor', axis=1, tiled=True)  40.1 us
    unnamed x1, blocking collectives  28.1 us
  transfers between devices with their start and end apart: 2, of which 1 were waited for; matrix products, arithmetic and copies ran while one was open for 1% of the time, Pallas kernels for 0%

commit v1 on v0

v1 whole, which is shorter than its diff:
```python
import functools
import math

import jax
import jax.numpy as jnp
import numpy as np
from jax import lax
from jax.experimental import pallas as pl
from jax.experimental.pallas import tpu as pltpu
from jax.sharding import PartitionSpec as P

HD = 128
RANK = 16
ADAPTER_SCALE = 2.0
ROPE_BASE = 500000.0
F32 = jnp.float32
BF16 = jnp.bfloat16
MESH = pl.DeviceIdType.MESH

NY, NZ = 4, 4
NT = NY * NZ * 2
HALF = NT // 2
T = 256
QC = 256
NC = 512


def rotary_tables():
    exponent = np.arange(HD // 2, dtype=np.float32) * np.float32(2.0 / HD)
    frequency = (1.0 / np.float32(ROPE_BASE) ** exponent).astype(np.float32)
    wavelength = (2.0 * math.pi / frequency).astype(np.float32)
    blend = (8192.0 / wavelength - 1.0) / 3.0
    middle = (1.0 - blend) * frequency / 8.0 + blend * frequency
    scaled = np.where(
        wavelength < 2048.0, frequency, np.where(wavelength > 8192.0, frequency / 8.0, middle)
    ).astype(np.float32)
    angle = np.arange(T, dtype=np.float32)[:, None] * scaled[None, :]
    cosine = np.cos(angle).astype(np.float32)
    sine = np.sin(angle).astype(np.float32)
    rows = np.stack(
        [np.concatenate([cosine, cosine], 1), np.concatenate([sine, -sine], 1)]
    )
    cols = np.stack([cosine.T, sine.T])
    return rows, cols


def nt(left, right):
    return lax.dot_general(left, right, (((1,), (1,)), ((), ())), preferred_element_type=F32)


def nn(left, right):
    return lax.dot_general(left, right, (((1,), (0,)), ((), ())), preferred_element_type=F32)


def tn(left, right):
    return lax.dot_general(left, right, (((0,), (0,)), ((), ())), preferred_element_type=F32)


def picks(rows, cols, first, offset):
    a = lax.broadcasted_iota(jnp.int32, (rows, cols), 0)
    col = lax.broadcasted_iota(jnp.int32, (rows, cols), 1)
    e = (a & 7) - first
    hit = (e >= 0) & (e < 2) & (col == offset + 2 * (a >> 3) + e)
    return jnp.where(hit, 1.0, 0.0).astype(BF16)


def kernel(
    ndp,
    normed_h, queries_h, keys_h, values_h, cot_h, seg_h, wq_h, wk_h, wv_h,
    adown_h, upq_h, upkv_h, accd_h, accq_h, acckv_h, tab_h, tabt_h,
    out_i, out_d, out_q, out_kv,
    normed, queries, cot, seg, wq, wkv, adown, upq, upkv, accd, accq, acckv, tab, tabt,
    kvown, kvt, rs_src, rs_dst, qall, kvg, ps_src, ps_in, ps_all, pay, dp_in, acc, bias,
    lsem, wsem, kvs, kvr, rss, rsr, qs, qr, gs, gr, pss, psr, pas, par, dps, dpr,
):
    i = lax.axis_index("tensor")
    b = lax.axis_index("dp")
    core = i % 2
    z = (i // 2) % NZ
    y = i // (2 * NZ)
    side = i // HALF
    own_in = core == side

    def dev(dy, dz, dc):
        return (((y + dy) % NY) * NZ + (z + dz) % NZ) * 2 + (core + dc) % 2

    loads = [
        (keys_h, kvown.at[0]), (values_h, kvown.at[1]), (queries_h.at[0], queries),
        (cot_h.at[0], cot), (seg_h, seg), (normed_h.at[0], normed), (adown_h, adown),
        (upq_h, upq), (upkv_h, upkv), (tab_h, tab), (tabt_h, tabt),
        (accd_h, accd), (accq_h, accq), (acckv_h, acckv), (wk_h, wkv.at[0]), (wv_h, wkv.at[1]),
    ]
    loads = [pltpu.make_async_copy(src, dst, lsem.at[n]) for n, (src, dst) in enumerate(loads)]
    for copy in loads:
        copy.start()

    barrier = pltpu.get_barrier_semaphore()

    def greet_t(k, _):
        pl.semaphore_signal(
            barrier, 1, device_id=(b, (i + 1 + k) % NT), device_id_type=MESH
        )
        return 0

    def greet_d(k, _):
        pl.semaphore_signal(
            barrier, 1, device_id=((b + 1 + k) % ndp, i), device_id_type=MESH
        )
        return 0

    lax.fori_loop(0, NT - 1, greet_t, 0)
    lax.fori_loop(0, ndp - 1, greet_d, 0)

    def load_w(k, _):
        pltpu.make_async_copy(
            wq_h.at[:, pl.ds(pl.multiple_of(k * QC, QC), QC)], wq.at[k], wsem
        ).start()
        return 0

    lax.fori_loop(0, NT, load_w, 0)

    def remote(src, dst, send, recv, to):
        return pltpu.make_async_remote_copy(
            src_ref=src, dst_ref=dst, send_sem=send, recv_sem=recv,
            device_id=to, device_id_type=MESH,
        )

    def drain(ref, sem):
        pltpu.make_async_copy(ref, ref, sem).wait()

    loads[0].wait()
    loads[1].wait()
    pl.semaphore_wait(barrier, NT - 1 + ndp - 1)

    home = pl.ds(pl.multiple_of((i % HALF) * 16, 16), 16)

    def send_kv(m, _):
        to = 2 * m + side

        @pl.when(to != i)
        def _():
            remote(kvown, kvt.at[:, home, :], kvs, kvr, (b, to)).start()

        return 0

    lax.fori_loop(0, HALF, send_kv, 0)

    @pl.when(own_in)
    def _():
        kvt[:, home, :] = kvown[...]

    loads[4].wait()
    doc = jnp.broadcast_to(seg[...].astype(F32), (T, T))
    row = lax.broadcasted_iota(jnp.int32, (T, T), 0)
    col = lax.broadcasted_iota(jnp.int32, (T, T), 1)
    bias[...] = jnp.where((col <= row) & (doc == doc.T), 0.0, -jnp.inf)
    loads[5].wait()
    loads[6].wait()
    down_part = nt(adown[...].reshape(3 * RANK, NC), normed[...])
    for n in range(2):
        ps_src[n, 64:112, :] = down_part[:, n * 128 : (n + 1) * 128]
        ps_src[n, 112:128, :] = jnp.zeros((16, 128), F32)
    for n in (2, 3, 7, 8, 9, 10):
        loads[n].wait()

    def wait_16(sem, part, whole):
        @pl.when(own_in)
        def _():
            drain(part, sem)

        @pl.when(jnp.logical_not(own_in))
        def _():
            drain(whole, sem)

    wait_16(kvr, kvt.at[:, 0:240, :], kvt)

    scale = 1.0 / math.sqrt(HD)
    for h in range(2):
        cols = slice(h * HD, (h + 1) * HD)
        q, g = queries[:, cols], cot[:, cols]
        kt, vt = kvt[0, cols, :], kvt[1, cols, :]
        scores = nn(q, kt) * scale + bias[...]
        weights = jnp.exp(scores - jnp.max(scores, axis=1, keepdims=True))
        weights = weights / jnp.sum(weights, axis=1, keepdims=True)
        weight_grad = nn(g, vt)
        delta = jnp.sum(weights * weight_grad, axis=1, keepdims=True)
        score_grad = (weights * (weight_grad - delta)).astype(BF16)
        query_rot = nt(score_grad, kt) * scale
        qall[i, :, cols] = (
            query_rot * tab[0] + pltpu.roll(query_rot, HD // 2, 1) * tab[1]
        ).astype(BF16)
        key_rot = tn(q, score_grad) * scale
        one, two = key_rot[: HD // 2], key_rot[HD // 2 :]
        cosine, sine = tabt[0], tabt[1]
        rs_src[0, cols, :] = jnp.concatenate(
            [one * cosine + two * sine, two * cosine - one * sine], axis=0
        ).astype(BF16)
        rs_src[1, cols, :] = tn(g, weights.astype(BF16)).astype(BF16)

    def send_rs(m, _):
        to = HALF * core + m

        @pl.when(to != i)
        def _():
            remote(
                rs_src.at[:, pl.ds(pl.multiple_of(16 * m, 16), 16), :],
                rs_dst.at[i // 2], rss, rsr, (b, to),
            ).start()

        return 0

    lax.fori_loop(0, HALF, send_rs, 0)

    @pl.when(own_in)
    def _():
        rs_dst[i // 2] = rs_src[:, home, :]

    def q_ref(slot, part):
        if part is None:
            return qall.at[slot]
        return qall.at[slot, pl.ds(part * (T // 2), T // 2), :]

    def g_ref(slot, part):
        rows = pl.ds(pl.multiple_of(slot * 16, 16), 16)
        if part is None:
            return kvg.at[:, rows, :]
        return kvg.at[part, rows, :]

    class Gather:
        def __init__(self, ref, send, recv):
            self.ref, self.s, self.r = ref, send, recv

        def push(self, slot, to, part=None):
            ref = self.ref(slot, part)
            remote(ref, ref, self.s, self.r.at[slot], (b, to)).start()

        def wait(self, slot):
            drain(self.ref(slot, None), self.r.at[slot])

        def first(self):
            own = dev(0, 0, 0)
            for to in (dev(0, 1, 0), dev(0, -1, 0), dev(1, 0, 0), dev(-1, 0, 0), dev(0, 0, 1)):
                self.push(own, to)

        def column(self, dz):
            slot = dev(0, dz, 0)
            self.wait(slot)
            if dz in (1, -1):
                self.push(slot, dev(0, -dz, 0), 0 if dz == -1 else 1)
            for to in (dev(1, 0, 0), dev(-1, 0, 0), dev(0, 0, 1)):
                self.push(slot, to)

        def spread(self, dz):
            for dy in (-1, 1):
                slot = dev(dy, dz, 0)
                self.wait(slot)
                self.push(slot, dev(-dy, 0, 0), 0 if dy == -1 else 1)
                self.push(slot, dev(0, 0, 1))

        def last(self, dz):
            slot = dev(2, dz, 0)
            self.wait(slot)
            self.push(slot, dev(0, 0, 1))

    query = Gather(q_ref, qs, qr)
    keyvalue = Gather(g_ref, gs, gr)
    query.first()

    up_rows = nn(picks(64, RANK, 0, 0), upq[...]).astype(BF16)
    up_part = nt(up_rows, qall[i])

    wait_16(rsr, rs_dst.at[0:15], rs_dst)
    total = rs_dst[0].astype(F32)
    for n in range(1, HALF):
        total = total + rs_dst[n].astype(F32)
    total = total.astype(BF16)
    mine = pl.ds(pl.multiple_of(i * 16, 16), 16)
    kvg[:, mine, :] = total
    keyvalue.first()
    for p in range(2):
        up_rows = nn(picks(64, RANK, 2 + 2 * p, 0), upkv[p]).astype(BF16)
        up_part = up_part + nn(up_rows, total[p])
    up_part = ADAPTER_SCALE * up_part
    for n in range(2):
        ps_src[n, 0:64, :] = up_part[:, n * 128 : (n + 1) * 128]

    def part_of(j):
        return j % 2, pl.ds(pl.multiple_of(8 * (j // 2), 8), 8)

    def send_ps(k, _):
        to = (i + 1 + k) % NT
        half, rows = part_of(to)
        remote(ps_src.at[half, rows, :], ps_in.at[i], pss, psr, (b, to)).start()
        return 0

    lax.fori_loop(0, NT - 1, send_ps, 0)
    my_half, my_rows = part_of(i)
    ps_in[i] = ps_src[my_half, my_rows, :]

    query.spread(0)
    query.column(-1)
    query.column(1)

    drain(wq, wsem)
    acc[...] = jnp.zeros_like(acc)

    def times(slot):
        acc[...] += nt(qall[slot], wq[slot])

    def project(dz):
        query.last(dz)

        def near(k, _):
            times(dev(k, dz, 0))
            return 0

        lax.fori_loop(0, NY, near, 0)

        def far(k, _):
            slot = dev(k, dz, 1)
            query.wait(slot)
            times(slot)
            return 0

        lax.fori_loop(0, NY, far, 0)

    drain(ps_in.at[0 : NT - 1], psr)
    ps_all[my_half, my_rows, :] = jnp.sum(ps_in[...], axis=0)

    def send_pa(k, _):
        to = (i + 1 + k) % NT
        ref = ps_all.at[my_half, my_rows, :]
        remote(ref, ref, pas, par, (b, to)).start()
        return 0

    lax.fori_loop(0, NT - 1, send_pa, 0)

    keyvalue.spread(0)
    keyvalue.column(-1)
    keyvalue.column(1)
    query.spread(-1)
    query.spread(1)
    query.column(2)
    project(0)
    keyvalue.last(0)
    keyvalue.spread(-1)
    keyvalue.spread(1)
    keyvalue.column(2)

    drain(ps_in.at[0 : NT - 1], par)
    sums = jnp.concatenate([ps_all[0], ps_all[1]], axis=1)
    up_sum = sums[0:64]
    down_half = sums[64:112].astype(BF16)
    high = up_sum.astype(BF16)
    rest = up_sum - high.astype(F32)
    middle = rest.astype(BF16)
    low = (rest - middle.astype(F32)).astype(BF16)
    down_grad = nn(high, normed[...]) + (nn(middle, normed[...]) + nn(low, normed[...]))
    downs = [
        nn(picks(64, 3 * RANK, 6, p * RANK), down_half).astype(BF16) for p in range(3)
    ]
    pay[...] = down_grad
    pay[:, 0:QC] += nn(downs[0], qall[i])
    for p in range(2):
        start = QC + p * 128
        pay[:, start : start + 16] += nt(downs[1 + p], kvg[p, mine, :])

    def send_dp(k, _):
        to = (b + 1 + k) % ndp
        remote(
            pay.at[pl.ds(pl.multiple_of(8 * to, 8), 8), :], dp_in.at[b], dps, dpr, (to, i)
        ).start()
        return 0

    lax.fori_loop(0, ndp - 1, send_dp, 0)
    dp_in[b] = pay[pl.ds(pl.multiple_of(8 * b, 8), 8), :]

    query.last(-1)
    query.last(1)
    query.spread(2)

    def project_rest(dz):
        def near(k, _):
            times(dev(k, dz, 0))
            return 0

        lax.fori_loop(0, NY, near, 0)

        def far(k, _):
            slot = dev(k, dz, 1)
            query.wait(slot)
            times(slot)
            return 0

        lax.fori_loop(0, NY, far, 0)

    project_rest(-1)
    project_rest(1)
    keyvalue.last(-1)
    keyvalue.last(1)
    keyvalue.spread(2)
    query.last(2)
    keyvalue.last(2)

    def far_kv(k, _):
        keyvalue.wait(2 * k + 1 - core)
        return 0

    lax.fori_loop(0, HALF, far_kv, 0)
    for n in (14, 15):
        loads[n].wait()
    adown_rows = nn(
        picks(64, 3 * RANK, 0, 0) + picks(64, 3 * RANK, 2, RANK) + picks(64, 3 * RANK, 4, 2 * RANK),
        adown[...].reshape(3 * RANK, NC),
    ).astype(BF16)
    for p in range(2):
        acc[...] += lax.dot_general(
            kvg[p], wkv[p], (((0,), (1,)), ((), ())), preferred_element_type=F32
        )
    acc[...] += tn(high, adown_rows)
    project_rest(2)
    out_i[0] = acc[...].astype(BF16)

    for n in (11, 12, 13):
        loads[n].wait()
    if ndp > 1:
        drain(dp_in.at[0 : ndp - 1], dpr)
    total = dp_in[0]
    for n in range(1, ndp):
        total = total + dp_in[n]
    tokens = float(ndp * T)
    for p in range(3):
        out_d[p] = accd[p] + total[2 * p : 2 * p + 2, :] / tokens
    out_q[...] = accq[...] + ADAPTER_SCALE * total[6:8, 0:QC] / tokens
    for p in range(2):
        start = QC + p * 128
        out_kv[p] = acckv[p] + ADAPTER_SCALE * total[6:8, start : start + 16] / tokens

    wait_16(kvs, kvt.at[:, 0:240, :], kvt)
    wait_16(rss, rs_dst.at[0:15], rs_dst)
    drain(qall.at[0 : NT - 1], qs)
    drain(kvg.at[:, 0 : 16 * (NT - 1), :], gs)
    drain(ps_in.at[0 : NT - 1], pss)
    drain(ps_in.at[0 : NT - 1], pas)
    if ndp > 1:
        drain(dp_in.at[0 : ndp - 1], dps)


def per_device(
    ndp, normed, queries, keys, values, context_grad, segments, w_query, w_key, w_value,
    adapter_down, up_query, up_keyvalue, accum_down, accum_query, accum_keyvalue,
):
    tab, tabt = rotary_tables()
    keys_t = jnp.transpose(keys[0])
    values_t = jnp.transpose(values[0])
    vmem = pltpu.VMEM
    dma = pltpu.SemaphoreType.DMA
    scratch = [
        vmem((T, NC), BF16),
        vmem((T, QC), BF16),
        vmem((T, QC), BF16),
        vmem((1, T), jnp.int32),
        vmem((NT, NC, QC), BF16),
        vmem((2, NC, 512), BF16),
        vmem((3, RANK, NC), BF16),
        vmem((RANK, QC), BF16),
        vmem((2, RANK, 16), BF16),
        vmem(accum_down.shape, F32),
        vmem(accum_query.shape, F32),
        vmem(accum_keyvalue.shape, F32),
        vmem(tab.shape, F32),
        vmem(tabt.shape, F32),
        vmem((2, 16, T), BF16),
        vmem((2, 2 * HD, T), BF16),
        vmem((2, 2 * HD, T), BF16),
        vmem((HALF, 2, 16, T), BF16),
        vmem((NT, T, QC), BF16),
        vmem((2, 512, T), BF16),
        vmem((2, 128, 128), F32),
        vmem((NT, 8, 128), F32),
        vmem((2, 128, 128), F32),
        vmem((64, NC), F32),
        vmem((8, 8, NC), F32),
        vmem((T, NC), F32),
        vmem((T, T), F32),
        dma((16,)), dma,
        dma, dma, dma, dma,
        dma, dma((NT,)), dma, dma((NT,)),
        dma, dma, dma, dma, dma, dma,
    ]
    out_shape = (
        jax.ShapeDtypeStruct((1, T, NC), BF16),
        jax.ShapeDtypeStruct(accum_down.shape, F32),
        jax.ShapeDtypeStruct(accum_query.shape, F32),
        jax.ShapeDtypeStruct(accum_keyvalue.shape, F32),
    )
    return pl.pallas_call(
        functools.partial(kernel, ndp),
        out_shape=out_shape,
        in_specs=[pl.BlockSpec(memory_space=pl.ANY)] * 17,
        out_specs=tuple(pl.BlockSpec(memory_space=pltpu.VMEM) for _ in out_shape),
        scratch_shapes=scratch,
        compiler_params=pltpu.CompilerParams(
            collective_id=0, has_side_effects=True, vmem_limit_bytes=64 * 1024 * 1024 - 288 * 1024
        ),
    )(
        normed, queries, keys_t, values_t, context_grad, segments, w_query, w_key, w_value,
        adapter_down, up_query, up_keyvalue, accum_down, accum_query, accum_keyvalue,
        jnp.asarray(tab), jnp.asarray(tabt),
    )


def solution(mesh):
    in_specs = (
        P("dp", None, "tensor"),
        P("dp", None, "tensor"),
        P("dp", None, "tensor"),
        P("dp", None, "tensor"),
        P("dp", None, "tensor"),
        P("dp", None),
        P("tensor", None),
        P("tensor", None),
        P("tensor", None),
        P(None, None, "tensor"),
        P(None, "tensor"),
        P(None, None, "tensor"),
        P(None, "dp", "tensor"),
        P("dp", "tensor"),
        P(None, "dp", "tensor"),
    )
    out_specs = (
        P("dp", None, "tensor"),
        P(None, "dp", "tensor"),
        P("dp", "tensor"),
        P(None, "dp", "tensor"),
    )
    return jax.shard_map(
        functools.partial(per_device, mesh.shape["dp"]),
        mesh=mesh, in_specs=in_specs, out_specs=out_specs, check_vma=False,
    )
```

time: 489 us -> 72.5 us (0.15)
  blocking collectives: 401 us -> 0 us
  Pallas kernels: 0 us -> 66.1 us
  waiting for transfers between devices: 43.8 us -> 0 us
  between operations: 16.5 us -> 0.65 us
  matrix products: 15.8 us -> 0 us
  other arithmetic: 5.12 us -> 0 us
    psum x2 -> x0, blocking collectives: 283 us -> none  [the longest x1 145 us: per_device(): key_sum, value_sum = lax.psum((key_flat, value_flat), 'tensor')]
    all_gather x2 -> x0, blocking collectives: 90.1 us -> none  [the longest x1 50 us: per_device(): lax.all_gather(keys[0], 'tensor', axis=1, tiled=True)]
    pallas_call x0 -> x1, Pallas kernels: none -> 66.1 us  [per_device(): pl.pallas_call(functools.partial(kernel, ndp), out_shape=out_shape, in_sp...]
    unnamed x3 -> x0, waiting for transfers between devices: 43.8 us -> none
    unnamed x1 -> x0, blocking collectives: 28.1 us -> none
    dot_general x20 -> x0, matrix products: 15.4 us -> none  [the longest x7 8.46 us: contract_last(): lax.dot_general(left, right, (((1,), (1,)), ((), ())), preferred_element_...]
  transfers between devices with their start and end apart: 2 -> 0, of which waited for: 1 -> 0; matrix products, arithmetic and copies ran while one was open for 1% -> 0% of each run, Pallas kernels for 0% -> 0%
where the time goes in v1:
time: 72.5 us; the launch traced here: 72.3 us
  Pallas kernels  66.1 us (91%)
  local copies, waits for them, and re-layouts  5.49 us (8%)
    pallas_call x1, Pallas kernels, per_device(): pl.pallas_call(functools.partial(kernel, ndp), out_shape=out_shape, in_sp...  66.1 us
    unnamed x4, local copies, waits for them, and re-layouts  5.49 us

profile of v1, /device:TPU:1, one launch (start us, length us, event | category | flops | bytes accessed | tf_op | source)
XLA Modules:
  0.0 72.3 jit_solution(2451435143755596375)
XLA Ops:
  0.6 66.1 %shard_map.192 = (bf16[1,256,512]{2,1,0:T(8,128)(2,1)}, f32[3,2,512]{2,1,0:T(2,128)}, f32[2,256]{1,0:T(2,128)}, f32[2,2,16]{2,1,0:T(2,128)}) custom-call(bf16[1,256,512]{2,1,0:T(8,128)(2,1)} %normed_h.1, bf16[1,256,256]{2,1,0:T(8,128)(2,1)} %queries_h.1, bf16[16,256]{1,0:T(8,128)(2,1)} %bitcast.6, bf16[16,256]{1,0:T(8,128)(2,1)} %bitcast.7, ...), custom_call_target="tpu_custom_call" | custom-call | tf_op jit(solution)/shard_map/pallas_call | solution.py:497
  66.8 1.7 %copy.25 = bf16[1,256,512]{2,1,0:T(8,128)(2,1)} copy(bf16[1,256,512]{2,1,0:T(8,128)(2,1)} %get-tuple-element.8) | data formatting | bytes 524288
  68.5 1.3 %copy.26 = f32[3,2,512]{2,1,0:T(2,128)} copy(f32[3,2,512]{2,1,0:T(2,128)} %get-tuple-element.9) | data formatting | bytes 24576
  69.8 1.3 %copy.27 = f32[2,256]{1,0:T(2,128)} copy(f32[2,256]{1,0:T(2,128)} %get-tuple-element.10) | data formatting | bytes 4096
  71.0 1.3 %copy.28 = f32[2,2,16]{2,1,0:T(2,128)} copy(f32[2,2,16]{2,1,0:T(2,128)} %get-tuple-element.11) | data formatting | bytes 512

commit v2 on v1

v2 whole, which is shorter than its diff:
```python
import functools
import math

import jax
import jax.numpy as jnp
import numpy as np
from jax import lax
from jax.experimental import pallas as pl
from jax.experimental.pallas import tpu as pltpu
from jax.sharding import PartitionSpec as P

HD = 128
RANK = 16
ADAPTER_SCALE = 2.0
ROPE_BASE = 500000.0
F32 = jnp.float32
BF16 = jnp.bfloat16
MESH = pl.DeviceIdType.MESH

NY, NZ = 4, 4
NT = NY * NZ * 2
HALF = NT // 2
T = 256
QC = 256
NC = 512


def rotary_tables():
    exponent = np.arange(HD // 2, dtype=np.float32) * np.float32(2.0 / HD)
    frequency = (1.0 / np.float32(ROPE_BASE) ** exponent).astype(np.float32)
    wavelength = (2.0 * math.pi / frequency).astype(np.float32)
    blend = (8192.0 / wavelength - 1.0) / 3.0
    middle = (1.0 - blend) * frequency / 8.0 + blend * frequency
    scaled = np.where(
        wavelength < 2048.0, frequency, np.where(wavelength > 8192.0, frequency / 8.0, middle)
    ).astype(np.float32)
    angle = np.arange(T, dtype=np.float32)[:, None] * scaled[None, :]
    cosine = np.cos(angle).astype(np.float32)
    sine = np.sin(angle).astype(np.float32)
    rows = np.stack(
        [np.concatenate([cosine, cosine], 1), np.concatenate([sine, -sine], 1)]
    )
    cols = np.stack([cosine.T, sine.T])
    return rows, cols


def nt(left, right):
    return lax.dot_general(left, right, (((1,), (1,)), ((), ())), preferred_element_type=F32)


def nn(left, right):
    return lax.dot_general(left, right, (((1,), (0,)), ((), ())), preferred_element_type=F32)


def tn(left, right):
    return lax.dot_general(left, right, (((0,), (0,)), ((), ())), preferred_element_type=F32)


CHUNKS = ((0, 256, "z"),)

ORDER = (
    ("first", 0), ("up",), ("fwd", 0, 0), ("w",), ("mm", 0, 0), ("rsy",), ("spr", 0, 0, 1),
    ("spr", 0, 0, -1), ("fwd", 1, 0), ("fwd", -1, 0), ("mm", 1, 0), ("mm", -1, 0),
    ("col", 0, 1), ("col", 0, -1), ("fwd", 0, 1), ("fwd", 0, -1), ("fwd", 2, 0), ("mm", 0, 1),
    ("mm", 0, -1), ("mm", 2, 0), ("up2",), ("rsz",), ("first", "g"), ("gfwd", 0, 0),
    ("spr", 0, 1, 1), ("spr", 0, 1, -1), ("fwd", 1, 1), ("fwd", -1, 1), ("col", 0, 2),
    ("fwd", 0, 2), ("mm", 1, 1), ("mm", -1, 1), ("mm", 0, 2), ("spr", 0, -1, 1),
    ("spr", 0, -1, -1), ("col", "g", 1), ("col", "g", -1), ("gfwd", 0, 1), ("gfwd", 0, -1),
    ("spr", "g", 0, 1), ("spr", "g", 0, -1), ("gfwd", 1, 0), ("gfwd", -1, 0), ("fwd", 1, -1),
    ("fwd", -1, -1), ("fwd", 2, 1), ("mm", 1, -1), ("mm", -1, -1), ("dp",), ("col", "g", 2),
    ("gfwd", 0, 2), ("mm", 2, 1), ("spr", 0, 2, 1), ("spr", 0, 2, -1), ("fwd", 1, 2),
    ("fwd", -1, 2), ("fwd", 2, -1), ("spr", "g", 1, 1), ("spr", "g", 1, -1), ("gfwd", 1, 1),
    ("gfwd", -1, 1), ("spr", "g", -1, 1), ("spr", "g", -1, -1), ("gfwd", 2, 0), ("gfwd", 1, -1),
    ("spr", "g", 2, 1), ("spr", "g", 2, -1), ("gfwd", -1, -1), ("gfwd", 1, 2), ("gfwd", -1, 2),
    ("mm", 2, -1), ("mm", 1, 2), ("fwd", 2, 2), ("mm", -1, 2), ("gfwd", 2, 1), ("gfwd", 2, -1),
    ("gfwd", 2, 2), ("mm", 2, 2), ("dpout",), ("kv",),
)


def kernel(
    ndp,
    normed_h, queries_h, keys_h, values_h, cot_h, seg_h, wq_h, wk_h, wv_h,
    adown_h, upq_h, upkv_h, accd_h, accq_h, acckv_h, tab_h, tabt_h,
    out_i, out_d, out_q, out_kv,
    normed, queries, cot, seg, wq, wkv, adown, upq, upkv, accd, accq, acckv, tab, tabt,
    kvown, kt, vt, utown, ut, rs_src, rsy, rsz, rs_dst, qall, kvg, ps_src, ps_in, ps_all,
    pay, dp_in, acc, bias, ob, od, oq, okv,
    lsem, wsem, kvs, kvr, uts, utr, rys, ryr, rzs, rzr, qs, qr, fs, fr, gs, gr,
    pss, psr, pas, par, dps, dpr, osem,
):
    i = lax.axis_index("tensor")
    b = lax.axis_index("dp")
    core = i % 2
    z = (i // 2) % NZ
    y = i // (2 * NZ)
    side = i // HALF
    own_in = core == side

    def dev(dy, dz, dc):
        return (((y + dy) % NY) * NZ + (z + dz) % NZ) * 2 + (core + dc) % 2

    loads = [
        (keys_h, kvown.at[0]), (values_h, kvown.at[1]), (queries_h.at[0], queries),
        (cot_h.at[0], cot), (seg_h, seg), (normed_h.at[0], normed), (adown_h, adown),
        (upq_h, upq), (upkv_h, upkv), (tab_h, tab), (tabt_h, tabt),
        (accd_h, accd), (accq_h, accq), (acckv_h, acckv), (wk_h, wkv.at[0]), (wv_h, wkv.at[1]),
    ]
    loads = [pltpu.make_async_copy(src, dst, lsem.at[n]) for n, (src, dst) in enumerate(loads)]
    for copy in loads:
        copy.start()

    barrier = pltpu.get_barrier_semaphore()

    def greet_t(k, _):
        pl.semaphore_signal(
            barrier, 1, device_id=(b, (i + 1 + k) % NT), device_id_type=MESH
        )
        return 0

    def greet_d(k, _):
        pl.semaphore_signal(
            barrier, 1, device_id=((b + 1 + k) % ndp, i), device_id_type=MESH
        )
        return 0

    lax.fori_loop(0, NT - 1, greet_t, 0)
    lax.fori_loop(0, ndp - 1, greet_d, 0)

    def load_w(k, _):
        pltpu.make_async_copy(
            wq_h.at[:, pl.ds(pl.multiple_of(k * QC, QC), QC)], wq.at[k], wsem
        ).start()
        return 0

    lax.fori_loop(0, NT, load_w, 0)

    def remote(src, dst, send, recv, to):
        return pltpu.make_async_remote_copy(
            src_ref=src, dst_ref=dst, send_sem=send, recv_sem=recv,
            device_id=to, device_id_type=MESH,
        )

    def drain(ref, sem):
        pltpu.make_async_copy(ref, ref, sem).wait()

    def by(test, sem, part, whole):
        @pl.when(test)
        def _():
            drain(part, sem)

        @pl.when(jnp.logical_not(test))
        def _():
            drain(whole, sem)

    owner = (i < 24) & (core == (i // 2) % 2)

    class Sums:
        def __init__(self, k):
            self.src, self.into, self.all = ps_src.at[k], ps_in.at[k], ps_all.at[k]
            self.sems = pss.at[k], psr.at[k], pas.at[k], par.at[k]

        def piece(self, ref, n):
            return ref.at[n % 2, pl.ds(pl.multiple_of(8 * (n // 2), 8), 8), :]

        def scatter(self, value):
            for n in range(2):
                self.src[n] = value[:, n * 128 : (n + 1) * 128]

            def send(n, _):
                to = 2 * n + n % 2

                @pl.when(to != i)
                def _():
                    remote(
                        self.piece(self.src, n), self.into.at[i],
                        self.sems[0], self.sems[1], (b, to),
                    ).start()

                return 0

            lax.fori_loop(0, 12, send, 0)

        def reduce(self):
            @pl.when(owner)
            def _():
                n = i // 2
                rows = pl.ds(pl.multiple_of(8 * (n // 2), 8), 8)
                self.into[i] = self.src[n % 2, rows, :]
                drain(self.into.at[0 : NT - 1], self.sems[1])
                self.all[n % 2, rows, :] = jnp.sum(self.into[...], axis=0)

                def send(k, _):
                    ref = self.piece(self.all, n)
                    remote(
                        ref, ref, self.sems[2], self.sems[3], (b, (i + 1 + k) % NT)
                    ).start()
                    return 0

                lax.fori_loop(0, NT - 1, send, 0)

        def result(self):
            by(owner, self.sems[3], self.into.at[0:11], self.into.at[0:12])
            return jnp.concatenate([self.all[0], self.all[1]], axis=1)

        def finish(self):
            by(owner, self.sems[0], self.into.at[0:11], self.into.at[0:12])

            @pl.when(owner)
            def _():
                drain(self.into.at[0 : NT - 1], self.sems[2])

    downs, ups = Sums(0), Sums(1)

    loads[0].wait()
    loads[1].wait()
    pl.semaphore_wait(barrier, NT - 1 + ndp - 1)

    home = pl.ds(pl.multiple_of((i % HALF) * 16, 16), 16)

    def scatter_home(src, dst, send, recv):
        def one(m, _):
            to = 2 * m + side

            @pl.when(to != i)
            def _():
                remote(src, dst.at[home, :], send, recv, (b, to)).start()

            return 0

        lax.fori_loop(0, HALF, one, 0)

        @pl.when(own_in)
        def _():
            dst[home, :] = src[...]

    scatter_home(kvown.at[0], kt, kvs.at[0], kvr.at[0])
    scatter_home(kvown.at[1], vt, kvs.at[1], kvr.at[1])

    loads[5].wait()
    loads[6].wait()
    downs.scatter(nt(adown[...].reshape(3 * RANK, NC), normed[...]))
    loads[8].wait()
    rank = lax.broadcasted_iota(jnp.int32, (RANK, 128), 0)
    lane = lax.broadcasted_iota(jnp.int32, (RANK, 128), 1)
    columns = jnp.zeros((16, 128), F32)
    for p in range(2):
        place = jnp.where(lane == rank + p * RANK, 1.0, 0.0).astype(BF16)
        columns = columns + tn(upkv[p], place)
    utown[...] = columns.astype(BF16)
    scatter_home(utown, ut, uts, utr)
    loads[4].wait()
    doc = jnp.broadcast_to(seg[...].astype(F32), (T, T))
    row = lax.broadcasted_iota(jnp.int32, (T, T), 0)
    col = lax.broadcasted_iota(jnp.int32, (T, T), 1)
    bias[...] = jnp.where((col <= row) & (doc == doc.T), 0.0, -jnp.inf)
    acc[...] = jnp.zeros_like(acc)
    for n in (2, 3, 7, 9, 10):
        loads[n].wait()

    def send_rsy(p):
        for h in range(2):
            to = ((2 * core + h) * NZ + z) * 2 + core

            @pl.when(to != i)
            def _():
                remote(rs_src.at[p, h], rsy.at[p, y], rys.at[p], ryr.at[p], (b, to)).start()

            @pl.when(to == i)
            def _():
                rsy[p, y] = rs_src[p, h]

    scale = 1.0 / math.sqrt(HD)
    heads = [slice(0, HD), slice(HD, 2 * HD)]
    by(own_in, kvr.at[0], kt.at[0:240, :], kt)
    probs = []
    for h in heads:
        scores = nn(queries[:, h], kt[h, :]) * scale + bias[...]
        weights = jnp.exp(scores - jnp.max(scores, axis=1, keepdims=True))
        probs.append(weights / jnp.sum(weights, axis=1, keepdims=True))
    for n, h in enumerate(heads):
        rs_src[1, n] = tn(cot[:, h], probs[n].astype(BF16)).astype(BF16)
    send_rsy(1)
    by(own_in, kvr.at[1], vt.at[0:240, :], vt)
    score_grads = []
    cosine, sine = tabt[0], tabt[1]
    for n, h in enumerate(heads):
        weight_grad = nn(cot[:, h], vt[h, :])
        delta = jnp.sum(probs[n] * weight_grad, axis=1, keepdims=True)
        score_grads.append((probs[n] * (weight_grad - delta)).astype(BF16))
        key_rot = tn(queries[:, h], score_grads[n]) * scale
        one, two = key_rot[: HD // 2], key_rot[HD // 2 :]
        rs_src[0, n] = jnp.concatenate(
            [one * cosine + two * sine, two * cosine - one * sine], axis=0
        ).astype(BF16)
    send_rsy(0)
    for n, h in enumerate(heads):
        query_rot = nt(score_grads[n], kt[h, :]) * scale
        qall[i, :, h] = (
            query_rot * tab[0] + pltpu.roll(query_rot, HD // 2, 1) * tab[1]
        ).astype(BF16)

    class Gather:
        def __init__(self, axis, ref, send, recv):
            self.axis, self.ref, self.s, self.r = axis, ref, send, recv

        def at(self, d, e):
            return dev(e, d, 0) if self.axis == "z" else dev(d, e, 0)

        def push(self, slot, to, part=None):
            ref = self.ref(slot, part)
            remote(ref, ref, self.s, self.r.at[slot], (b, to)).start()

        def wait(self, slot):
            drain(self.ref(slot, None), self.r.at[slot])

        def first(self):
            for d, e in ((1, 0), (-1, 0), (0, 1), (0, -1)):
                self.push(i, self.at(d, e))

        def col(self, d):
            slot = self.at(d, 0)
            self.wait(slot)
            if d != 2:
                self.push(slot, self.at(-d, 0), 0 if d == -1 else 1)
            for e in (1, -1):
                self.push(slot, self.at(0, e))

        def spr(self, d, e):
            slot = self.at(d, e)
            self.wait(slot)
            self.push(slot, self.at(0, -e), 0 if e == -1 else 1)

        def far(self, dy, dz):
            if (dy if self.axis == "z" else dz) == 2:
                self.wait(dev(dy, dz, 0))

    def q_ref(first, last):
        half = (last - first) // 2

        def ref(slot, part):
            if part is None:
                return qall.at[slot, pl.ds(first, last - first), :]
            return qall.at[slot, pl.ds(first + part * half, half), :]

        return ref

    def g_ref(slot, part):
        rows = pl.ds(pl.multiple_of(slot * 16, 16), 16)
        if part is None:
            return kvg.at[:, rows, :]
        return kvg.at[part, rows, :]

    gathers = {
        n: Gather(axis, q_ref(first, last), qs.at[n], qr.at[n])
        for n, (first, last, axis) in enumerate(CHUNKS)
    }
    gathers["g"] = Gather("z", g_ref, gs.at[0], gr)
    mine = pl.ds(pl.multiple_of(i * 16, 16), 16)
    other = i + 1 - 2 * core

    def step_first(tag):
        gathers[tag].first()

    def step_col(tag, d):
        gathers[tag].col(d)

    def step_spr(tag, d, e):
        gathers[tag].spr(d, e)

    def step_fwd(dy, dz):
        slot = dev(dy, dz, 0)
        for n in range(len(CHUNKS)):
            gathers[n].far(dy, dz)
        remote(qall.at[slot], qall.at[slot], fs, fr.at[slot], (b, other)).start()

    def step_gfwd(dy, dz):
        gathers["g"].far(dy, dz)
        ref = g_ref(dev(dy, dz, 0), None)
        remote(ref, ref, gs.at[1], gr.at[dev(dy, dz, 0)], (b, other)).start()

    def step_mm(dy, dz):
        one, two = dev(dy, dz, 0), dev(dy, dz, 1)
        drain(qall.at[two], fr.at[two])
        acc[...] += nt(qall[one], wq[one]) + nt(qall[two], wq[two])

    def step_up():
        by(own_in, utr, ut.at[0:240, :], ut)
        sums = [nt(upq[...], qall[i])]
        for p in range(2):
            part = rs_src[p].reshape(2 * HD, T)
            sums.append(tn(ut[...], part)[p * RANK : (p + 1) * RANK])
        ups.scatter(ADAPTER_SCALE * jnp.concatenate(sums, axis=0))
        downs.reduce()

    def step_up2():
        ups.reduce()

    def step_rsy():
        @pl.when(own_in)
        def _():
            for p in (1, 0):
                drain(rsy.at[p, 0 : NY - 1], ryr.at[p])
                total = rsy[p, 0].astype(F32)
                for n in range(1, NY):
                    total = total + rsy[p, n].astype(F32)
                rsz[p] = total.astype(BF16)

            def send(m, _):
                to = y * (2 * NZ) + m
                rows = pl.ds(pl.multiple_of(16 * m, 16), 16)

                @pl.when(to != i)
                def _():
                    remote(rsz.at[:, rows, :], rs_dst.at[z], rzs, rzr, (b, to)).start()

                return 0

            lax.fori_loop(0, 2 * NZ, send, 0)
            rs_dst[z] = rsz[:, pl.ds(pl.multiple_of(16 * (2 * z + core), 16), 16), :]

    def step_rsz():
        by(own_in, rzr, rs_dst.at[0 : NZ - 1], rs_dst)
        total = rs_dst[0].astype(F32)
        for n in range(1, NZ):
            total = total + rs_dst[n].astype(F32)
        kvg[:, mine, :] = total.astype(BF16)

    def step_dp():
        up_sum = ups.result()
        down_half = downs.result().astype(BF16)
        high = up_sum.astype(BF16)
        rest = up_sum - high.astype(F32)
        middle = rest.astype(BF16)
        low = (rest - middle.astype(F32)).astype(BF16)
        split = jnp.concatenate([high, middle, low], axis=0)
        grads = nn(split, normed[...])
        grad_down = grads[0:48] + (grads[48:96] + grads[96:144])
        grad_query = nn(down_half[0:RANK], qall[i])
        grad_kv = [
            nt(down_half[(1 + p) * RANK : (2 + p) * RANK], kvg[p, mine, :]) for p in range(2)
        ]
        for d in range(8):
            for p in range(3):
                pay[8 * d + 2 * p : 8 * d + 2 * p + 2, :] = grad_down[
                    p * RANK + 2 * d : p * RANK + 2 * d + 2
                ]
            pay[8 * d + 6 : 8 * d + 8, 0:QC] = grad_query[2 * d : 2 * d + 2]
            for p in range(2):
                start = QC + p * 128
                pay[8 * d + 6 : 8 * d + 8, start : start + 16] = grad_kv[p][2 * d : 2 * d + 2]

        def send(k, _):
            to = (b + 1 + k) % ndp
            remote(
                pay.at[pl.ds(pl.multiple_of(8 * to, 8), 8), :], dp_in.at[b], dps, dpr, (to, i)
            ).start()
            return 0

        lax.fori_loop(0, ndp - 1, send, 0)
        dp_in[b] = pay[pl.ds(pl.multiple_of(8 * b, 8), 8), :]
        acc[...] += tn(high, adown[...].reshape(3 * RANK, NC))

    stores = [
        pltpu.make_async_copy(src, dst, osem.at[n])
        for n, (src, dst) in enumerate(((ob, out_i.at[0]), (od, out_d), (oq, out_q), (okv, out_kv)))
    ]

    def step_dpout():
        for n in (11, 12, 13):
            loads[n].wait()
        if ndp > 1:
            drain(dp_in.at[0 : ndp - 1], dpr)
        total = dp_in[0]
        for n in range(1, ndp):
            total = total + dp_in[n]
        tokens = float(ndp * T)
        for p in range(3):
            od[p] = accd[p] + total[2 * p : 2 * p + 2, :] / tokens
        oq[...] = accq[...] + ADAPTER_SCALE * total[6:8, 0:QC] / tokens
        for p in range(2):
            start = QC + p * 128
            okv[p] = acckv[p] + ADAPTER_SCALE * total[6:8, start : start + 16] / tokens
        for copy in stores[1:]:
            copy.start()

    def step_kv():
        def far_kv(k, _):
            slot = 2 * k + 1 - core
            drain(g_ref(slot, None), gr.at[slot])
            return 0

        lax.fori_loop(0, HALF, far_kv, 0)
        for p in range(2):
            acc[...] += lax.dot_general(
                kvg[p], wkv[p], (((0,), (1,)), ((), ())), preferred_element_type=F32
            )

    def step_w():
        drain(wq, wsem)
        for n in (14, 15):
            loads[n].wait()

    steps = {
        "first": step_first, "col": step_col, "spr": step_spr, "fwd": step_fwd,
        "gfwd": step_gfwd, "mm": step_mm, "up": step_up, "up2": step_up2,
        "rsy": step_rsy, "rsz": step_rsz, "dp": step_dp, "dpout": step_dpout, "kv": step_kv,
        "w": step_w,
    }
    for name, *rest in ORDER:
        steps[name](*rest)
    ob[...] = acc[...].astype(BF16)
    stores[0].start()

    for n in range(2):
        by(own_in, kvs.at[n], kt.at[0:240, :], kt)
        by(own_in, rys.at[n], rs_src.at[n, 0], rs_src.at[n])
    by(own_in, uts, ut.at[0:240, :], ut)

    @pl.when(own_in)
    def _():
        drain(rsz.at[:, 0:112, :], rzs)

    for n, (first, last, _) in enumerate(CHUNKS):
        drain(qall.at[0:15, pl.ds(first, last - first), :], qs.at[n])
    drain(qall.at[0:16], fs)
    drain(kvg.at[:, 0:240, :], gs.at[0])
    drain(kvg.at[:, 0:256, :], gs.at[1])
    downs.finish()
    ups.finish()
    if ndp > 1:
        drain(dp_in.at[0 : ndp - 1], dps)
    for copy in stores:
        copy.wait()


def hand_over(*refs):
    copies = [
        pltpu.make_async_copy(refs[n], refs[4 + n], refs[8].at[n]) for n in range(4)
    ]
    for copy in copies:
        copy.start()
    for copy in copies:
        copy.wait()


def per_device(
    ndp, normed, queries, keys, values, context_grad, segments, w_query, w_key, w_value,
    adapter_down, up_query, up_keyvalue, accum_down, accum_query, accum_keyvalue,
):
    tab, tabt = rotary_tables()
    keys_t = jnp.transpose(keys[0])
    values_t = jnp.transpose(values[0])
    vmem = pltpu.VMEM
    dma = pltpu.SemaphoreType.DMA
    scratch = [
        vmem((T, NC), BF16),
        vmem((T, QC), BF16),
        vmem((T, QC), BF16),
        vmem((1, T), jnp.int32),
        vmem((NT, NC, QC), BF16),
        vmem((2, NC, 512), BF16),
        vmem((3, RANK, NC), BF16),
        vmem((RANK, QC), BF16),
        vmem((2, RANK, 16), BF16),
        vmem(accum_down.shape, F32),
        vmem(accum_query.shape, F32),
        vmem(accum_keyvalue.shape, F32),
        vmem(tab.shape, F32),
        vmem(tabt.shape, F32),
        vmem((2, 16, T), BF16),
        vmem((2 * HD, T), BF16),
        vmem((2 * HD, T), BF16),
        vmem((16, 128), BF16),
        vmem((2 * HD, 128), BF16),
        vmem((2, 2, HD, T), BF16),
        vmem((2, NY, HD, T), BF16),
        vmem((2, HD, T), BF16),
        vmem((NZ, 2, 16, T), BF16),
        vmem((NT, T, QC), BF16),
        vmem((2, 512, T), BF16),
        vmem((2, 2, 48, 128), F32),
        vmem((2, NT, 8, 128), F32),
        vmem((2, 2, 48, 128), F32),
        vmem((64, NC), F32),
        vmem((8, 8, NC), F32),
        vmem((T, NC), F32),
        vmem((T, T), F32),
        vmem((T, NC), BF16),
        vmem(accum_down.shape, F32),
        vmem(accum_query.shape, F32),
        vmem(accum_keyvalue.shape, F32),
        dma((16,)), dma,
        dma((2,)), dma((2,)), dma, dma, dma((2,)), dma((2,)), dma, dma,
        dma((len(CHUNKS),)), dma((len(CHUNKS), NT)), dma, dma((NT,)), dma((2,)), dma((NT,)),
        dma((2,)), dma((2,)), dma((2,)), dma((2,)), dma, dma, dma((4,)),
    ]
    out_shape = (
        jax.ShapeDtypeStruct((1, T, NC), BF16),
        jax.ShapeDtypeStruct(accum_down.shape, F32),
        jax.ShapeDtypeStruct(accum_query.shape, F32),
        jax.ShapeDtypeStruct(accum_keyvalue.shape, F32),
    )
    results = pl.pallas_call(
        functools.partial(kernel, ndp),
        out_shape=out_shape,
        in_specs=[pl.BlockSpec(memory_space=pl.ANY)] * 17,
        out_specs=tuple(pl.BlockSpec(memory_space=pl.ANY) for _ in out_shape),
        scratch_shapes=scratch,
        compiler_params=pltpu.CompilerParams(
            collective_id=0, has_side_effects=True, vmem_limit_bytes=64 * 1024 * 1024
        ),
    )(
        normed, queries, keys_t, values_t, context_grad, segments, w_query, w_key, w_value,
        adapter_down, up_query, up_keyvalue, accum_down, accum_query, accum_keyvalue,
        jnp.asarray(tab), jnp.asarray(tabt),
    )
    return pl.pallas_call(
        hand_over,
        out_shape=out_shape,
        in_specs=[pl.BlockSpec(memory_space=pltpu.VMEM)] * 4,
        out_specs=tuple(pl.BlockSpec(memory_space=pl.ANY) for _ in out_shape),
        scratch_shapes=[dma((4,))],
        compiler_params=pltpu.CompilerParams(vmem_limit_bytes=64 * 1024 * 1024),
    )(*results)


def solution(mesh):
    in_specs = (
        P("dp", None, "tensor"),
        P("dp", None, "tensor"),
        P("dp", None, "tensor"),
        P("dp", None, "tensor"),
        P("dp", None, "tensor"),
        P("dp", None),
        P("tensor", None),
        P("tensor", None),
        P("tensor", None),
        P(None, None, "tensor"),
        P(None, "tensor"),
        P(None, None, "tensor"),
        P(None, "dp", "tensor"),
        P("dp", "tensor"),
        P(None, "dp", "tensor"),
    )
    out_specs = (
        P("dp", None, "tensor"),
        P(None, "dp", "tensor"),
        P("dp", "tensor"),
        P(None, "dp", "tensor"),
    )
    return jax.shard_map(
        functools.partial(per_device, mesh.shape["dp"]),
        mesh=mesh, in_specs=in_specs, out_specs=out_specs, check_vma=False,
    )
```

time: 72.5 us -> 59.4 us (0.82)
  Pallas kernels: 66.1 us -> 58.7 us
  local copies, waits for them, and re-layouts: 5.49 us -> 0 us
    pallas_call x1, Pallas kernels: 66.1 us -> 57 us  [per_device(): pl.pallas_call(functools.partial(kernel, ndp), out_shape=out_shape, in_sp...]
    unnamed x4 -> x0, local copies, waits for them, and re-layouts: 5.49 us -> none
    pallas_call x0 -> x1, Pallas kernels: none -> 1.71 us  [per_device(): pl.pallas_call(hand_over, out_shape=out_shape, in_specs=[pl.BlockSpec(mem...]
where the time goes in v2:
time: 59.4 us; the launch traced here: 59.3 us
  Pallas kernels  58.7 us (99%)
  between operations  0.65 us (1%)
    pallas_call x1, Pallas kernels, per_device(): pl.pallas_call(functools.partial(kernel, ndp), out_shape=out_shape, in_sp...  57 us
    pallas_call x1, Pallas kernels, per_device(): pl.pallas_call(hand_over, out_shape=out_shape, in_specs=[pl.BlockSpec(mem...  1.71 us

profile of v2, /device:TPU:1, one launch (start us, length us, event | category | flops | bytes accessed | tf_op | source)
XLA Modules:
  0.0 59.3 jit_solution(3937123148281492874)
XLA Ops:
  0.6 57.0 %shard_map.192 = (bf16[1,256,512]{2,1,0:T(8,128)(2,1)}, f32[3,2,512]{2,1,0:T(2,128)}, f32[2,256]{1,0:T(2,128)}, f32[2,2,16]{2,1,0:T(2,128)}) custom-call(bf16[1,256,512]{2,1,0:T(8,128)(2,1)} %normed_h.1, bf16[1,256,256]{2,1,0:T(8,128)(2,1)} %queries_h.1, bf16[16,256]{1,0:T(8,128)(2,1)} %bitcast.6, bf16[16,256]{1,0:T(8,128)(2,1)} %bitcast.7, ...), custom_call_target="tpu_custom_call" | custom-call | tf_op jit(solution)/shard_map/pallas_call | solution.py:603
  57.6 1.7 %shard_map.193 = (bf16[1,256,512]{2,1,0:T(8,128)(2,1)}, f32[3,2,512]{2,1,0:T(2,128)}, f32[2,256]{1,0:T(2,128)}, f32[2,2,16]{2,1,0:T(2,128)}) custom-call(bf16[1,256,512]{2,1,0:T(8,128)(2,1)} %get-tuple-element.8.refs_0_, f32[3,2,512]{2,1,0:T(2,128)} %get-tuple-element.9.refs_1_, f32[2,256]{1,0:T(2,128)} %get-tuple-element.10.refs_2_, ...), custom_call_target="tpu_custom_call" | custom-call | tf_op jit(solution)/shard_map/pallas_call | solution.py:617

commit v3 on v2

v3 whole, which is shorter than its diff:
```python
import functools
import math

import jax
import jax.numpy as jnp
import numpy as np
from jax import lax
from jax.experimental import pallas as pl
from jax.experimental.pallas import tpu as pltpu
from jax.sharding import PartitionSpec as P

HD = 128
RANK = 16
ADAPTER_SCALE = 2.0
ROPE_BASE = 500000.0
F32 = jnp.float32
BF16 = jnp.bfloat16
MESH = pl.DeviceIdType.MESH

NY, NZ = 4, 4
NT = NY * NZ * 2
HALF = NT // 2
T = 256
QC = 256
NC = 512


def rotary_tables():
    exponent = np.arange(HD // 2, dtype=np.float32) * np.float32(2.0 / HD)
    frequency = (1.0 / np.float32(ROPE_BASE) ** exponent).astype(np.float32)
    wavelength = (2.0 * math.pi / frequency).astype(np.float32)
    blend = (8192.0 / wavelength - 1.0) / 3.0
    middle = (1.0 - blend) * frequency / 8.0 + blend * frequency
    scaled = np.where(
        wavelength < 2048.0, frequency, np.where(wavelength > 8192.0, frequency / 8.0, middle)
    ).astype(np.float32)
    angle = np.arange(T, dtype=np.float32)[:, None] * scaled[None, :]
    cosine = np.cos(angle).astype(np.float32)
    sine = np.sin(angle).astype(np.float32)
    rows = np.stack(
        [np.concatenate([cosine, cosine], 1), np.concatenate([sine, -sine], 1)]
    )
    cols = np.stack([cosine.T, sine.T])
    return rows, cols


def nt(left, right):
    return lax.dot_general(left, right, (((1,), (1,)), ((), ())), preferred_element_type=F32)


def nn(left, right):
    return lax.dot_general(left, right, (((1,), (0,)), ((), ())), preferred_element_type=F32)


def tn(left, right):
    return lax.dot_general(left, right, (((0,), (0,)), ((), ())), preferred_element_type=F32)


CHUNKS = ((0, 128, "z"), (128, 224, "z"), (224, 256, "y"))

FAR = (
    (2, 2), (2, 1), (2, -1), (1, 2), (-1, 2), (0, 2), (1, 1), (1, -1), (-1, 1), (-1, -1),
    (2, 0), (0, 1), (0, -1), (1, 0), (-1, 0), (0, 0),
)

ORDER = (
    ("first", 1), ("first", 2), ("up",), ("fwd", 0, 0), ("w",), ("mm", 0, 0), ("spr", 0, 0, 1),
    ("spr", 0, 0, -1), ("col", 0, 1), ("col", 0, -1), ("rsy", 1), ("col", 1, 1), ("col", 1, -1),
    ("rsy", 0), ("spr", 1, 0, 1), ("spr", 1, 0, -1), ("spr", 2, 0, 1), ("spr", 2, 0, -1),
    ("fwd", 0, 1), ("fwd", 0, -1), ("col", 2, 1), ("col", 2, -1), ("fwd", 1, 0), ("fwd", -1, 0),
    ("mm", 0, 1), ("mm", 0, -1), ("mm", 1, 0), ("col", 0, 2), ("mm", -1, 0), ("spr", 0, 1, 1),
    ("spr", 0, 1, -1), ("up2",), ("col", 1, 2), ("spr", 0, -1, 1), ("spr", 0, -1, -1),
    ("rsz", 1), ("gfirst", 1), ("fwd", 0, 2), ("spr", 1, 1, 1), ("spr", 1, 1, -1),
    ("spr", 2, 1, 1), ("spr", 2, 1, -1), ("fwd", 1, 1), ("rsz", 0), ("gfirst", 0),
    ("spr", 1, -1, 1), ("spr", 1, -1, -1), ("spr", 2, -1, 1), ("spr", 2, -1, -1),
    ("fwd", -1, 1), ("fwd", 1, -1), ("fwd", -1, -1), ("mm", 0, 2), ("col", 2, 2), ("fwd", 2, 0),
    ("mm", 1, 1), ("mm", -1, 1), ("gcol", 1, 1), ("gcol", 1, -1), ("spr", 0, 2, 1),
    ("spr", 0, 2, -1), ("mm", 1, -1), ("mm", -1, -1), ("mm", 2, 0), ("gcol", 0, 1),
    ("gcol", 0, -1), ("gcol", 1, 2), ("spr", 2, 2, 1), ("spr", 2, 2, -1), ("spr", 1, 2, 1),
    ("spr", 1, 2, -1), ("fwd", 1, 2), ("fwd", -1, 2), ("gcol", 0, 2), ("mm", 1, 2),
    ("fwd", 2, 1), ("mm", -1, 2), ("dp",), ("gfwd", 1, 0), ("fwd", 2, -1), ("mm", 2, 1),
    ("gfwd", 0, 0), ("mm", 2, -1), ("gfwd", 1, 1), ("gfwd", 1, -1), ("fwd", 2, 2),
    ("gfwd", 0, 1), ("gfwd", 0, -1), ("gfwd", 1, 2), ("mm", 2, 2), ("gfwd", 0, 2), ("kv", 1),
    ("kv", 0), ("dpout",),
)


def kernel(
    ndp,
    normed_h, queries_h, keys_h, values_h, cot_h, seg_h, wq_h, wk_h, wv_h,
    adown_h, upq_h, upkv_h, accd_h, accq_h, acckv_h, tab_h, tabt_h,
    out_i, out_d, out_q, out_kv,
    normed, queries, cot, seg, wq, wkv, adown, upq, upkv, accd, accq, acckv, tab, tabt,
    kvown, kt, vt, utown, ut, rs_src, rsy, rsz, rs_dst, qall, kvg, ps_src, ps_in, ps_all,
    pay, dp_in, acc, bias, ob, od, oq, okv,
    lsem, wsem, kvs, kvr, zs, zr, ys, yr, rys, ryr, rzs, rzr, qs, qr, fs, fr, gs, gr,
    pss, psr, pas, par, dps, dpr, osem,
):
    i = lax.axis_index("tensor")
    b = lax.axis_index("dp")
    core = i % 2
    z = (i // 2) % NZ
    y = i // (2 * NZ)
    side = i // HALF
    own_in = core == side

    def dev(dy, dz, dc):
        return (((y + dy) % NY) * NZ + (z + dz) % NZ) * 2 + (core + dc) % 2

    loads = [
        (keys_h, kvown.at[0]), (values_h, kvown.at[1]), (queries_h.at[0], queries),
        (cot_h.at[0], cot), (seg_h, seg), (normed_h.at[0], normed), (adown_h, adown),
        (upq_h, upq), (upkv_h, upkv), (tab_h, tab), (tabt_h, tabt),
        (accd_h, accd), (accq_h, accq), (acckv_h, acckv), (wk_h, wkv.at[0]), (wv_h, wkv.at[1]),
    ]
    loads = [pltpu.make_async_copy(src, dst, lsem.at[n]) for n, (src, dst) in enumerate(loads)]
    barrier = pltpu.get_barrier_semaphore()

    def greet_t(k, _):
        pl.semaphore_signal(
            barrier, 1, device_id=(b, (i + 1 + k) % NT), device_id_type=MESH
        )
        return 0

    def greet_d(k, _):
        pl.semaphore_signal(
            barrier, 1, device_id=((b + 1 + k) % ndp, i), device_id_type=MESH
        )
        return 0

    lax.fori_loop(0, NT - 1, greet_t, 0)
    lax.fori_loop(0, ndp - 1, greet_d, 0)
    for copy in loads:
        copy.start()

    def load_w(k, _):
        pltpu.make_async_copy(
            wq_h.at[:, pl.ds(pl.multiple_of(k * QC, QC), QC)], wq.at[k], wsem
        ).start()
        return 0

    def remote(src, dst, send, recv, to):
        return pltpu.make_async_remote_copy(
            src_ref=src, dst_ref=dst, send_sem=send, recv_sem=recv,
            device_id=to, device_id_type=MESH,
        )

    def drain(ref, sem):
        pltpu.make_async_copy(ref, ref, sem).wait()

    def by(test, sem, part, whole):
        @pl.when(test)
        def _():
            drain(part, sem)

        @pl.when(jnp.logical_not(test))
        def _():
            drain(whole, sem)

    owner = (i < 24) & (core == (i // 2) % 2)

    def piece(ref, n):
        return ref.at[n % 2, pl.ds(pl.multiple_of(16 * (n // 2), 16), 16), :]

    def scatter_sums():
        def send(k, _):
            n = (k % 3) * NZ + (z + 2 + k // 3) % NZ
            to = 2 * n + n % 2

            @pl.when(to != i)
            def _():
                remote(piece(ps_src, n), ps_in.at[i], pss, psr, (b, to)).start()

            return 0

        lax.fori_loop(0, 12, send, 0)

    def reduce_sums():
        @pl.when(owner)
        def _():
            n = i // 2
            rows = pl.ds(pl.multiple_of(16 * (n // 2), 16), 16)
            ps_in[i] = ps_src[n % 2, rows, :]
            drain(ps_in.at[0 : NT - 1], psr)
            ps_all[n % 2, rows, :] = jnp.sum(ps_in[...].astype(F32), axis=0).astype(BF16)

            def send(k, _):
                ref = piece(ps_all, n)
                remote(ref, ref, pas, par, (b, (i + 1 + k) % NT)).start()
                return 0

            lax.fori_loop(0, NT - 1, send, 0)

    loads[0].wait()
    loads[1].wait()
    loads[8].wait()
    rank = lax.broadcasted_iota(jnp.int32, (RANK, 128), 0)
    lane = lax.broadcasted_iota(jnp.int32, (RANK, 128), 1)
    columns = jnp.zeros((16, 128), F32)
    for p in range(2):
        place = jnp.where(lane == rank + p * RANK, 1.0, 0.0).astype(BF16)
        columns = columns + tn(upkv[p], place)
    utown[...] = columns.astype(BF16)
    pl.semaphore_wait(barrier, NT - 1 + ndp - 1)

    home = pl.ds(pl.multiple_of((i % HALF) * 16, 16), 16)

    def scatter_home(src, dst, send, recv, lanes=slice(None)):
        for dy, dz in FAR:
            to = dev(dy, dz, side - core)

            def start():
                remote(
                    src.at[:, lanes], dst.at[home, lanes], send, recv, (b, to)
                ).start()

            if (dy, dz) == (0, 0):
                pl.when(to != i)(start)
            else:
                start()

        @pl.when(own_in)
        def _():
            dst[home, lanes] = src[:, lanes]

    my_row = pl.ds(pl.multiple_of((y % 2) * HD, HD), HD)

    def along_z(src, dst, n, lanes):
        for dz in (2, 1, -1, 0):
            to = dev(0, dz, side - core)

            def start():
                remote(
                    src.at[:, lanes], dst.at[home, lanes], zs.at[n], zr.at[n], (b, to)
                ).start()

            if dz == 0:
                pl.when(to != i)(start)
            else:
                start()

        @pl.when(own_in)
        def _():
            dst[home, lanes] = src[:, lanes]

    def along_y(dst, n, lanes):
        @pl.when(own_in)
        def _():
            drain(dst.at[0:112, lanes], zr.at[n])
            for dy in (2, 1, -1):
                ref = dst.at[my_row, lanes]
                remote(ref, ref, ys.at[n], yr.at[n], (b, dev(dy, 0, 0))).start()

    early, late = slice(0, T // 2), slice(T // 2, T)
    along_z(kvown.at[1], vt, 0, late)
    along_z(utown, ut, 1, slice(None))
    scatter_home(kvown.at[0], kt, kvs.at[0], kvr.at[0], early)
    scatter_home(kvown.at[1], vt, kvs.at[1], kvr.at[1], early)
    scatter_home(kvown.at[0], kt, kvs.at[2], kvr.at[2], late)

    loads[5].wait()
    loads[6].wait()
    down_part = nt(adown[...].reshape(3 * RANK, NC), normed[...]).astype(BF16)
    for n in range(2):
        ps_src[n, 48:96, :] = down_part[:, n * 128 : (n + 1) * 128]
    loads[4].wait()
    doc = jnp.broadcast_to(seg[...].astype(F32), (T, T))
    row = lax.broadcasted_iota(jnp.int32, (T, T), 0)
    col = lax.broadcasted_iota(jnp.int32, (T, T), 1)
    bias[...] = jnp.where((col <= row) & (doc == doc.T), 0.0, -jnp.inf)
    acc[...] = jnp.zeros_like(acc)
    lax.fori_loop(0, NT, load_w, 0)
    for n in (2, 3, 7, 9, 10):
        loads[n].wait()

    class Gather:
        def __init__(self, axis, ref, send, recv):
            self.axis, self.ref, self.s, self.r = axis, ref, send, recv

        def at(self, d, e):
            return dev(e, d, 0) if self.axis == "z" else dev(d, e, 0)

        def push(self, slot, to, part=None):
            ref = self.ref(slot, part)
            remote(ref, ref, self.s, self.r.at[slot], (b, to)).start()

        def wait(self, slot):
            drain(self.ref(slot, None), self.r.at[slot])

        def first(self):
            for d, e in ((1, 0), (-1, 0), (0, 1), (0, -1)):
                self.push(i, self.at(d, e))

        def col(self, d):
            slot = self.at(d, 0)
            self.wait(slot)
            if d != 2:
                self.push(slot, self.at(-d, 0), 0 if d == -1 else 1)
            for e in (1, -1):
                self.push(slot, self.at(0, e))

        def spr(self, d, e):
            slot = self.at(d, e)
            self.wait(slot)
            self.push(slot, self.at(0, -e), 0 if e == -1 else 1)

        def far(self, dy, dz):
            if (dy if self.axis == "z" else dz) == 2:
                self.wait(dev(dy, dz, 0))

    def q_ref(first, last):
        half = (last - first) // 2

        def ref(slot, part):
            if part is None:
                return qall.at[slot, pl.ds(first, last - first), :]
            return qall.at[slot, pl.ds(first + part * half, half), :]

        return ref

    def g_ref(p, slot):
        return kvg.at[p, pl.ds(pl.multiple_of(slot * 16, 16), 16), :]

    gathers = {
        n: Gather(axis, q_ref(first, last), qs.at[n], qr.at[n])
        for n, (first, last, axis) in enumerate(CHUNKS)
    }
    mine = pl.ds(pl.multiple_of(i * 16, 16), 16)
    other = i + 1 - 2 * core

    def send_rsy(p, h):
        to = ((2 * core + h) * NZ + z) * 2 + core

        @pl.when(to != i)
        def _():
            remote(rs_src.at[p, h], rsy.at[p, y], rys.at[p], ryr.at[p], (b, to)).start()

        @pl.when(to == i)
        def _():
            rsy[p, y] = rs_src[p, h]

    def wait_home(n, ref, lanes):
        by(own_in, kvr.at[n], ref.at[0:240, lanes], ref.at[:, lanes])

    scale = 1.0 / math.sqrt(HD)
    heads = [slice(0, HD), slice(HD, 2 * HD)]
    cosine, sine = tabt[0], tabt[1]

    def softmax(h, rows, keys):
        scores = nn(queries[rows, h], kt[h, keys]) * scale + bias[rows, keys]
        weights = jnp.exp(scores - jnp.max(scores, axis=1, keepdims=True))
        return weights / jnp.sum(weights, axis=1, keepdims=True)

    def score_cotangent(h, rows, keys, weights):
        weight_grad = nn(cot[rows, h], vt[h, keys])
        delta = jnp.sum(weights * weight_grad, axis=1, keepdims=True)
        return (weights * (weight_grad - delta)).astype(BF16)

    def query_cotangent(h, rows, keys, score_grad):
        rot = nt(score_grad, kt[h, keys]) * scale
        qall[i, rows, h] = (
            rot * tab[0, rows, :] + pltpu.roll(rot, HD // 2, 1) * tab[1, rows, :]
        ).astype(BF16)

    def both(left, one, two):
        top = tn(left[early], one)
        rest = tn(left[late], two)
        return jnp.concatenate([rest[:, early] + top, rest[:, late]], axis=1)

    every = slice(0, T)
    wait_home(0, kt, early)
    along_y(vt, 0, late)
    along_y(ut, 1, slice(None))
    probs_early = [softmax(h, early, early) for h in heads]
    wait_home(1, vt, early)
    grads_early = []
    for n, h in enumerate(heads):
        grads_early.append(score_cotangent(h, early, early, probs_early[n]))
        query_cotangent(h, early, early, grads_early[n])
    gathers[0].first()
    wait_home(2, kt, late)
    probs = []
    for n, h in enumerate(heads):
        probs.append(softmax(h, late, every))
        rs_src[1, n] = both(
            cot[:, h], probs_early[n].astype(BF16), probs[n].astype(BF16)
        ).astype(BF16)
        send_rsy(1, n)
    by(own_in, yr.at[0], vt.at[0:HD, late], vt.at[:, late])
    grads = []
    for n, h in enumerate(heads):
        grads.append(score_cotangent(h, late, every, probs[n]))
        key_rot = both(queries[:, h], grads_early[n], grads[n]) * scale
        one, two = key_rot[: HD // 2], key_rot[HD // 2 :]
        rs_src[0, n] = jnp.concatenate(
            [one * cosine + two * sine, two * cosine - one * sine], axis=0
        ).astype(BF16)
        send_rsy(0, n)
    for n, h in enumerate(heads):
        query_cotangent(h, late, every, grads[n])

    def step_first(tag):
        gathers[tag].first()

    def step_col(tag, d):
        gathers[tag].col(d)

    def step_spr(tag, d, e):
        gathers[tag].spr(d, e)

    def step_fwd(dy, dz):
        slot = dev(dy, dz, 0)
        for n in range(len(CHUNKS)):
            gathers[n].far(dy, dz)
        remote(qall.at[slot], qall.at[slot], fs, fr.at[slot], (b, other)).start()

    def push_g(p, slot, to):
        ref = g_ref(p, slot)
        remote(ref, ref, gs.at[p], gr.at[p, slot], (b, to)).start()

    def wait_g(p, slot):
        drain(g_ref(p, slot), gr.at[p, slot])

    def step_gfirst(p):
        for dy, dz in ((0, 2), (0, 1), (0, -1), (2, 0), (1, 0), (-1, 0)):
            push_g(p, i, dev(dy, dz, 0))

    def step_gcol(p, dz):
        wait_g(p, dev(0, dz, 0))
        for dy in (2, 1, -1):
            push_g(p, dev(0, dz, 0), dev(dy, 0, 0))

    def step_gfwd(p, dz):
        for dy in (0, 1, -1, 2):
            slot = dev(dy, dz, 0)
            if dy != 0:
                wait_g(p, slot)
            ref = g_ref(p, slot)
            remote(ref, ref, gs.at[2 + p], gr.at[p, slot], (b, other)).start()

    def step_mm(dy, dz):
        one, two = dev(dy, dz, 0), dev(dy, dz, 1)
        drain(qall.at[two], fr.at[two])
        acc[...] += nt(qall[one], wq[one]) + nt(qall[two], wq[two])

    def step_up():
        by(own_in, yr.at[1], ut.at[0:HD, :], ut)
        sums = [nt(upq[...], qall[i])]
        for p in range(2):
            part = rs_src[p].reshape(2 * HD, T)
            sums.append(tn(ut[...], part)[p * RANK : (p + 1) * RANK])
        up_part = (ADAPTER_SCALE * jnp.concatenate(sums, axis=0)).astype(BF16)
        for n in range(2):
            ps_src[n, 0:48, :] = up_part[:, n * 128 : (n + 1) * 128]
        scatter_sums()

    def step_up2():
        reduce_sums()

    def step_rsy(p):
        @pl.when(own_in)
        def _():
            drain(rsy.at[p, 0 : NY - 1], ryr.at[p])
            total = rsy[p, 0].astype(F32)
            for n in range(1, NY):
                total = total + rsy[p, n].astype(F32)
            rsz[p] = total.astype(BF16)
            for dz in (2, 1, -1, 0):
                for dc in range(2):
                    to = dev(0, dz, dc)
                    rows = pl.ds(pl.multiple_of(16 * (to % (2 * NZ)), 16), 16)
                    if (dz, dc) == (0, 0):
                        rs_dst[p, z] = rsz[p, rows, :]
                    else:
                        remote(
                            rsz.at[p, rows, :], rs_dst.at[p, z], rzs.at[p], rzr.at[p], (b, to)
                        ).start()

    def step_rsz(p):
        by(own_in, rzr.at[p], rs_dst.at[p, 0 : NZ - 1], rs_dst.at[p])
        total = rs_dst[p, 0].astype(F32)
        for n in range(1, NZ):
            total = total + rs_dst[p, n].astype(F32)
        kvg[p, mine, :] = total.astype(BF16)

    def step_dp():
        by(owner, par, ps_in.at[0:11], ps_in.at[0:12])
        sums = jnp.concatenate([ps_all[0], ps_all[1]], axis=1)
        up_half, down_half = sums[0:48], sums[48:96]
        grad_down = nn(up_half, normed[...])
        grad_query = nn(down_half[0:RANK], qall[i])
        grad_kv = [
            nt(down_half[(1 + p) * RANK : (2 + p) * RANK], kvg[p, mine, :]) for p in range(2)
        ]
        for d in range(8):
            for p in range(3):
                pay[8 * d + 2 * p : 8 * d + 2 * p + 2, :] = grad_down[
                    p * RANK + 2 * d : p * RANK + 2 * d + 2
                ]
            pay[8 * d + 6 : 8 * d + 8, 0:QC] = grad_query[2 * d : 2 * d + 2]
            for p in range(2):
                start = QC + p * 128
                pay[8 * d + 6 : 8 * d + 8, start : start + 16] = grad_kv[p][2 * d : 2 * d + 2]

        def send(k, _):
            to = (b + 1 + k) % ndp
            remote(
                pay.at[pl.ds(pl.multiple_of(8 * to, 8), 8), :], dp_in.at[b], dps, dpr, (to, i)
            ).start()
            return 0

        lax.fori_loop(0, ndp - 1, send, 0)
        dp_in[b] = pay[pl.ds(pl.multiple_of(8 * b, 8), 8), :]
        acc[...] += tn(up_half, adown[...].reshape(3 * RANK, NC))

    stores = [
        pltpu.make_async_copy(src, dst, osem.at[n])
        for n, (src, dst) in enumerate(((ob, out_i.at[0]), (od, out_d), (oq, out_q), (okv, out_kv)))
    ]

    def step_dpout():
        for n in (11, 12, 13):
            loads[n].wait()
        if ndp > 1:
            drain(dp_in.at[0 : ndp - 1], dpr)
        total = dp_in[0]
        for n in range(1, ndp):
            total = total + dp_in[n]
        tokens = float(ndp * T)
        for p in range(3):
            od[p] = accd[p] + total[2 * p : 2 * p + 2, :] / tokens
        oq[...] = accq[...] + ADAPTER_SCALE * total[6:8, 0:QC] / tokens
        for p in range(2):
            start = QC + p * 128
            okv[p] = acckv[p] + ADAPTER_SCALE * total[6:8, start : start + 16] / tokens
        for copy in stores[1:]:
            copy.start()

    def step_kv(p):
        def far_kv(k, _):
            wait_g(p, 2 * k + 1 - core)
            return 0

        lax.fori_loop(0, HALF, far_kv, 0)
        acc[...] += lax.dot_general(
            kvg[p], wkv[p], (((0,), (1,)), ((), ())), preferred_element_type=F32
        )

    def step_w():
        drain(wq, wsem)
        for n in (14, 15):
            loads[n].wait()

    steps = {
        "first": step_first, "col": step_col, "spr": step_spr, "fwd": step_fwd,
        "gfirst": step_gfirst, "gcol": step_gcol, "gfwd": step_gfwd, "mm": step_mm, "up": step_up, "up2": step_up2,
        "rsy": step_rsy, "rsz": step_rsz, "dp": step_dp, "dpout": step_dpout, "kv": step_kv,
        "w": step_w,
    }
    for name, *rest in ORDER:
        steps[name](*rest)
    ob[...] = acc[...].astype(BF16)
    stores[0].start()

    for n in range(3):
        by(own_in, kvs.at[n], kt.at[0:240, early], kt.at[:, early])
    for n, lanes in enumerate((late, slice(None))):
        ref = (vt, ut)[n]
        by(own_in, zs.at[n], ref.at[0:48, lanes], ref.at[0:64, lanes])

        @pl.when(own_in)
        def _():
            drain(qall.at[0, 0:192, :], ys.at[n])

    for p in range(2):
        by(own_in, rys.at[p], rs_src.at[p, 0], rs_src.at[p])

        @pl.when(own_in)
        def _():
            drain(rsz.at[p, 0:112, :], rzs.at[p])

        drain(kvg.at[p, 0:240, :], gs.at[p])
        drain(kvg.at[p, 0:256, :], gs.at[2 + p])
    for n, (first, last, _) in enumerate(CHUNKS):
        drain(qall.at[0:15, pl.ds(first, last - first), :], qs.at[n])
    drain(qall.at[0:16], fs)
    by(owner, pss, ps_in.at[0:11], ps_in.at[0:12])

    @pl.when(owner)
    def _():
        drain(ps_in.at[0 : NT - 1], pas)

    if ndp > 1:
        drain(dp_in.at[0 : ndp - 1], dps)
    for copy in stores:
        copy.wait()


def hand_over(*refs):
    copies = [
        pltpu.make_async_copy(refs[n], refs[4 + n], refs[8].at[n]) for n in range(4)
    ]
    for copy in copies:
        copy.start()
    for copy in copies:
        copy.wait()


def per_device(
    ndp, normed, queries, keys, values, context_grad, segments, w_query, w_key, w_value,
    adapter_down, up_query, up_keyvalue, accum_down, accum_query, accum_keyvalue,
):
    tab, tabt = rotary_tables()
    keys_t = jnp.transpose(keys[0])
    values_t = jnp.transpose(values[0])
    vmem = pltpu.VMEM
    dma = pltpu.SemaphoreType.DMA
    scratch = [
        vmem((T, NC), BF16),
        vmem((T, QC), BF16),
        vmem((T, QC), BF16),
        vmem((1, T), jnp.int32),
        vmem((NT, NC, QC), BF16),
        vmem((2, NC, 512), BF16),
        vmem((3, RANK, NC), BF16),
        vmem((RANK, QC), BF16),
        vmem((2, RANK, 16), BF16),
        vmem(accum_down.shape, F32),
        vmem(accum_query.shape, F32),
        vmem(accum_keyvalue.shape, F32),
        vmem(tab.shape, F32),
        vmem(tabt.shape, F32),
        vmem((2, 16, T), BF16),
        vmem((2 * HD, T), BF16),
        vmem((2 * HD, T), BF16),
        vmem((16, 128), BF16),
        vmem((2 * HD, 128), BF16),
        vmem((2, 2, HD, T), BF16),
        vmem((2, NY, HD, T), BF16),
        vmem((2, HD, T), BF16),
        vmem((2, NZ, 16, T), BF16),
        vmem((NT, T, QC), BF16),
        vmem((2, 512, T), BF16),
        vmem((2, 96, 128), BF16),
        vmem((NT, 16, 128), BF16),
        vmem((2, 96, 128), BF16),
        vmem((64, NC), F32),
        vmem((8, 8, NC), F32),
        vmem((T, NC), F32),
        vmem((T, T), F32),
        vmem((T, NC), BF16),
        vmem(accum_down.shape, F32),
        vmem(accum_query.shape, F32),
        vmem(accum_keyvalue.shape, F32),
        dma((16,)), dma,
        dma((3,)), dma((3,)), dma((2,)), dma((2,)), dma((2,)), dma((2,)),
        dma((2,)), dma((2,)), dma((2,)), dma((2,)),
        dma((len(CHUNKS),)), dma((len(CHUNKS), NT)), dma, dma((NT,)), dma((4,)), dma((2, NT)),
        dma, dma, dma, dma, dma, dma, dma((4,)),
    ]
    out_shape = (
        jax.ShapeDtypeStruct((1, T, NC), BF16),
        jax.ShapeDtypeStruct(accum_down.shape, F32),
        jax.ShapeDtypeStruct(accum_query.shape, F32),
        jax.ShapeDtypeStruct(accum_keyvalue.shape, F32),
    )
    results = pl.pallas_call(
        functools.partial(kernel, ndp),
        out_shape=out_shape,
        in_specs=[pl.BlockSpec(memory_space=pl.ANY)] * 17,
        out_specs=tuple(pl.BlockSpec(memory_space=pl.ANY) for _ in out_shape),
        scratch_shapes=scratch,
        compiler_params=pltpu.CompilerParams(
            collective_id=0, has_side_effects=True, vmem_limit_bytes=64 * 1024 * 1024
        ),
    )(
        normed, queries, keys_t, values_t, context_grad, segments, w_query, w_key, w_value,
        adapter_down, up_query, up_keyvalue, accum_down, accum_query, accum_keyvalue,
        jnp.asarray(tab), jnp.asarray(tabt),
    )
    return pl.pallas_call(
        hand_over,
        out_shape=out_shape,
        in_specs=[pl.BlockSpec(memory_space=pltpu.VMEM)] * 4,
        out_specs=tuple(pl.BlockSpec(memory_space=pl.ANY) for _ in out_shape),
        scratch_shapes=[dma((4,))],
        compiler_params=pltpu.CompilerParams(vmem_limit_bytes=64 * 1024 * 1024),
    )(*results)


def solution(mesh):
    in_specs = (
        P("dp", None, "tensor"),
        P("dp", None, "tensor"),
        P("dp", None, "tensor"),
        P("dp", None, "tensor"),
        P("dp", None, "tensor"),
        P("dp", None),
        P("tensor", None),
        P("tensor", None),
        P("tensor", None),
        P(None, None, "tensor"),
        P(None, "tensor"),
        P(None, None, "tensor"),
        P(None, "dp", "tensor"),
        P("dp", "tensor"),
        P(None, "dp", "tensor"),
    )
    out_specs = (
        P("dp", None, "tensor"),
        P(None, "dp", "tensor"),
        P("dp", "tensor"),
        P(None, "dp", "tensor"),
    )
    return jax.shard_map(
        functools.partial(per_device, mesh.shape["dp"]),
        mesh=mesh, in_specs=in_specs, out_specs=out_specs, check_vma=False,
    )
```

time: 59.4 us -> 52.6 us (0.89)
  Pallas kernels: 58.7 us -> 51.8 us
    pallas_call x1, Pallas kernels: 57 us -> 50.1 us  [per_device(): pl.pallas_call(functools.partial(kernel, ndp), out_shape=out_shape, in_sp...]
where the time goes in v3:
time: 52.6 us; the launch traced here: 52.4 us
  Pallas kernels  51.8 us (98%)
  between operations  0.65 us (1%)
    pallas_call x1, Pallas kernels, per_device(): pl.pallas_call(functools.partial(kernel, ndp), out_shape=out_shape, in_sp...  50.1 us
    pallas_call x1, Pallas kernels, per_device(): pl.pallas_call(hand_over, out_shape=out_shape, in_specs=[pl.BlockSpec(mem...  1.71 us

profile of v3, /device:TPU:1, one launch (start us, length us, event | category | flops | bytes accessed | tf_op | source)
XLA Modules:
  0.0 52.4 jit_solution(11229441605940698985)
XLA Ops:
  0.6 50.1 %shard_map.192 = (bf16[1,256,512]{2,1,0:T(8,128)(2,1)}, f32[3,2,512]{2,1,0:T(2,128)}, f32[2,256]{1,0:T(2,128)}, f32[2,2,16]{2,1,0:T(2,128)}) custom-call(bf16[1,256,512]{2,1,0:T(8,128)(2,1)} %normed_h.1, bf16[1,256,256]{2,1,0:T(8,128)(2,1)} %queries_h.1, bf16[16,256]{1,0:T(8,128)(2,1)} %bitcast.6, bf16[16,256]{1,0:T(8,128)(2,1)} %bitcast.7, ...), custom_call_target="tpu_custom_call" | custom-call | tf_op jit(solution)/shard_map/pallas_call | solution.py:667
  50.7 1.7 %shard_map.193 = (bf16[1,256,512]{2,1,0:T(8,128)(2,1)}, f32[3,2,512]{2,1,0:T(2,128)}, f32[2,256]{1,0:T(2,128)}, f32[2,2,16]{2,1,0:T(2,128)}) custom-call(bf16[1,256,512]{2,1,0:T(8,128)(2,1)} %get-tuple-element.8.refs_0_, f32[3,2,512]{2,1,0:T(2,128)} %get-tuple-element.9.refs_1_, f32[2,256]{1,0:T(2,128)} %get-tuple-element.10.refs_2_, ...), custom_call_target="tpu_custom_call" | custom-call | tf_op jit(solution)/shard_map/pallas_call | solution.py:681

commit v4 on v3

--- a/solution.py
+++ b/solution.py
@@ -92,9 +92,9 @@
     out_i, out_d, out_q, out_kv,
     normed, queries, cot, seg, wq, wkv, adown, upq, upkv, accd, accq, acckv, tab, tabt,
     kvown, kt, vt, utown, ut, rs_src, rsy, rsz, rs_dst, qall, kvg, ps_src, ps_in, ps_all,
-    pay, dp_in, acc, bias, ob, od, oq, okv,
+    pay, dp_in, acc, bias,
     lsem, wsem, kvs, kvr, zs, zr, ys, yr, rys, ryr, rzs, rzr, qs, qr, fs, fr, gs, gr,
-    pss, psr, pas, par, dps, dpr, osem,
+    pss, psr, pas, par, dps, dpr,
 ):
     i = lax.axis_index("tensor")
     b = lax.axis_index("dp")
@@ -116,21 +116,22 @@
     loads = [pltpu.make_async_copy(src, dst, lsem.at[n]) for n, (src, dst) in enumerate(loads)]
     barrier = pltpu.get_barrier_semaphore()
 
-    def greet_t(k, _):
-        pl.semaphore_signal(
-            barrier, 1, device_id=(b, (i + 1 + k) % NT), device_id_type=MESH
-        )
+    def greet(to):
+        pl.semaphore_signal(barrier, 1, device_id=to, device_id_type=MESH)
+
+    def greet_d(k, _):
+        greet(((b + 1 + k) % ndp, i))
         return 0
 
-    def greet_d(k, _):
-        pl.semaphore_signal(
-            barrier, 1, device_id=((b + 1 + k) % ndp, i), device_id_type=MESH
-        )
-        return 0
-
-    lax.fori_loop(0, NT - 1, greet_t, 0)
-    lax.fori_loop(0, ndp - 1, greet_d, 0)
-    for copy in loads:
+    for copy in loads[:2]:
+        copy.start()
+    for n, (dy, dz) in enumerate(FAR):
+        for dc in (1, 0):
+            if (dy, dz, dc) != (0, 0, 0):
+                greet((b, dev(dy, dz, dc)))
+        if n == 6:
+            lax.fori_loop(0, ndp - 1, greet_d, 0)
+    for copy in loads[2:]:
         copy.start()
 
     def load_w(k, _):
@@ -193,6 +194,61 @@
 
     loads[0].wait()
     loads[1].wait()
+    pl.semaphore_wait(barrier, NT - 1 + ndp - 1)
+
+    home = pl.ds(pl.multiple_of((i % HALF) * 16, 16), 16)
+
+    def scatter_home(src, dst, send, recv, lanes=slice(None)):
+        for dy, dz in FAR:
+            to = dev(dy, dz, side - core)
+
+            def start():
+                remote(
+                    src.at[:, lanes], dst.at[home, lanes], send, recv, (b, to)
+                ).start()
+
+            if (dy, dz) == (0, 0):
+                pl.when(to != i)(start)
+            else:
+                start()
+
+        @pl.when(own_in)
+        def _():
+            dst[home, lanes] = src[:, lanes]
+
+    my_row = pl.ds(pl.multiple_of((y % 2) * HD, HD), HD)
+
+    def along_z(src, dst, n, lanes):
+        for dz in (2, 1, -1, 0):
+            to = dev(0, dz, side - core)
+
+            def start():
+                remote(
+                    src.at[:, lanes], dst.at[home, lanes], zs.at[n], zr.at[n], (b, to)
+                ).start()
+
+            if dz == 0:
+                pl.when(to != i)(start)
+            else:
+                start()
+
+        @pl.when(own_in)
+        def _():
+            dst[home, lanes] = src[:, lanes]
+
+    def along_y(dst, n, lanes):
+        @pl.when(own_in)
+        def _():
+            drain(dst.at[0:112, lanes], zr.at[n])
+            for dy in (2, 1, -1):
+                ref = dst.at[my_row, lanes]
+                remote(ref, ref, ys.at[n], yr.at[n], (b, dev(dy, 0, 0))).start()
+
+    early, late = slice(0, T // 2), slice(T // 2, T)
+    along_z(kvown.at[1], vt, 0, late)
+    scatter_home(kvown.at[0], kt, kvs.at[0], kvr.at[0], early)
+    scatter_home(kvown.at[1], vt, kvs.at[1], kvr.at[1], early)
+    scatter_home(kvown.at[0], kt, kvs.at[2], kvr.at[2], late)
     loads[8].wait()
     rank = lax.broadcasted_iota(jnp.int32, (RANK, 128), 0)
     lane = lax.broadcasted_iota(jnp.int32, (RANK, 128), 1)
@@ -201,62 +257,7 @@
         place = jnp.where(lane == rank + p * RANK, 1.0, 0.0).astype(BF16)
         columns = columns + tn(upkv[p], place)
     utown[...] = columns.astype(BF16)
-    pl.semaphore_wait(barrier, NT - 1 + ndp - 1)
-
-    home = pl.ds(pl.multiple_of((i % HALF) * 16, 16), 16)
-
-    def scatter_home(src, dst, send, recv, lanes=slice(None)):
-        for dy, dz in FAR:
-            to = dev(dy, dz, side - core)
-
-            def start():
-                remote(
-                    src.at[:, lanes], dst.at[home, lanes], send, recv, (b, to)
-                ).start()
-
-            if (dy, dz) == (0, 0):
-                pl.when(to != i)(start)
-            else:
-                start()
-
-        @pl.when(own_in)
-        def _():
-            dst[home, lanes] = src[:, lanes]
-
-    my_row = pl.ds(pl.multiple_of((y % 2) * HD, HD), HD)
-
-    def along_z(src, dst, n, lanes):
-        for dz in (2, 1, -1, 0):
-            to = dev(0, dz, side - core)
-
-            def start():
-                remote(
-                    src.at[:, lanes], dst.at[home, lanes], zs.at[n], zr.at[n], (b, to)
-                ).start()
-
-            if dz == 0:
-                pl.when(to != i)(start)
-            else:
-                start()
-
-        @pl.when(own_in)
-        def _():
-            dst[home, lanes] = src[:, lanes]
-
-    def along_y(dst, n, lanes):
-        @pl.when(own_in)
-        def _():
-            drain(dst.at[0:112, lanes], zr.at[n])
-            for dy in (2, 1, -1):
-                ref = dst.at[my_row, lanes]
-                remote(ref, ref, ys.at[n], yr.at[n], (b, dev(dy, 0, 0))).start()
-
-    early, late = slice(0, T // 2), slice(T // 2, T)
-    along_z(kvown.at[1], vt, 0, late)
     along_z(utown, ut, 1, slice(None))
-    scatter_home(kvown.at[0], kt, kvs.at[0], kvr.at[0], early)
-    scatter_home(kvown.at[1], vt, kvs.at[1], kvr.at[1], early)
-    scatter_home(kvown.at[0], kt, kvs.at[2], kvr.at[2], late)
 
     loads[5].wait()
     loads[6].wait()
@@ -269,7 +270,6 @@
     col = lax.broadcasted_iota(jnp.int32, (T, T), 1)
     bias[...] = jnp.where((col <= row) & (doc == doc.T), 0.0, -jnp.inf)
     acc[...] = jnp.zeros_like(acc)
-    lax.fori_loop(0, NT, load_w, 0)
     for n in (2, 3, 7, 9, 10):
         loads[n].wait()
 
@@ -370,7 +370,6 @@
     every = slice(0, T)
     wait_home(0, kt, early)
     along_y(vt, 0, late)
-    along_y(ut, 1, slice(None))
     probs_early = [softmax(h, early, early) for h in heads]
     wait_home(1, vt, early)
     grads_early = []
@@ -378,6 +377,7 @@
         grads_early.append(score_cotangent(h, early, early, probs_early[n]))
         query_cotangent(h, early, early, grads_early[n])
     gathers[0].first()
+    along_y(ut, 1, slice(None))
     wait_home(2, kt, late)
     probs = []
     for n, h in enumerate(heads):
@@ -398,6 +398,7 @@
         send_rsy(0, n)
     for n, h in enumerate(heads):
         query_cotangent(h, late, every, grads[n])
+    lax.fori_loop(0, NT, load_w, 0)
 
     def step_first(tag):
         gathers[tag].first()
@@ -513,11 +514,6 @@
         dp_in[b] = pay[pl.ds(pl.multiple_of(8 * b, 8), 8), :]
         acc[...] += tn(up_half, adown[...].reshape(3 * RANK, NC))
 
-    stores = [
-        pltpu.make_async_copy(src, dst, osem.at[n])
-        for n, (src, dst) in enumerate(((ob, out_i.at[0]), (od, out_d), (oq, out_q), (okv, out_kv)))
-    ]
-
     def step_dpout():
         for n in (11, 12, 13):
             loads[n].wait()
@@ -528,13 +524,11 @@
             total = total + dp_in[n]
         tokens = float(ndp * T)
         for p in range(3):
-            od[p] = accd[p] + total[2 * p : 2 * p + 2, :] / tokens
-        oq[...] = accq[...] + ADAPTER_SCALE * total[6:8, 0:QC] / tokens
+            out_d[p] = accd[p] + total[2 * p : 2 * p + 2, :] / tokens
+        out_q[...] = accq[...] + ADAPTER_SCALE * total[6:8, 0:QC] / tokens
         for p in range(2):
             start = QC + p * 128
-            okv[p] = acckv[p] + ADAPTER_SCALE * total[6:8, start : start + 16] / tokens
-        for copy in stores[1:]:
-            copy.start()
+            out_kv[p] = acckv[p] + ADAPTER_SCALE * total[6:8, start : start + 16] / tokens
 
     def step_kv(p):
         def far_kv(k, _):
@@ -559,8 +553,7 @@
     }
     for name, *rest in ORDER:
         steps[name](*rest)
-    ob[...] = acc[...].astype(BF16)
-    stores[0].start()
+    out_i[0] = acc[...].astype(BF16)
 
     for n in range(3):
         by(own_in, kvs.at[n], kt.at[0:240, early], kt.at[:, early])
@@ -592,8 +585,6 @@
 
     if ndp > 1:
         drain(dp_in.at[0 : ndp - 1], dps)
-    for copy in stores:
-        copy.wait()
 
 
 def hand_over(*refs):
@@ -648,15 +639,11 @@
         vmem((8, 8, NC), F32),
         vmem((T, NC), F32),
         vmem((T, T), F32),
-        vmem((T, NC), BF16),
-        vmem(accum_down.shape, F32),
-        vmem(accum_query.shape, F32),
-        vmem(accum_keyvalue.shape, F32),
         dma((16,)), dma,
         dma((3,)), dma((3,)), dma((2,)), dma((2,)), dma((2,)), dma((2,)),
         dma((2,)), dma((2,)), dma((2,)), dma((2,)),
         dma((len(CHUNKS),)), dma((len(CHUNKS), NT)), dma, dma((NT,)), dma((4,)), dma((2, NT)),
-        dma, dma, dma, dma, dma, dma, dma((4,)),
+        dma, dma, dma, dma, dma, dma,
     ]
     out_shape = (
         jax.ShapeDtypeStruct((1, T, NC), BF16),
@@ -666,12 +653,12 @@
     )
     results = pl.pallas_call(
         functools.partial(kernel, ndp),
-        out_shape=out_shape,
+        out_shape=tuple(pltpu.VMEM(o.shape, o.dtype) for o in out_shape),
         in_specs=[pl.BlockSpec(memory_space=pl.ANY)] * 17,
-        out_specs=tuple(pl.BlockSpec(memory_space=pl.ANY) for _ in out_shape),
+        out_specs=tuple(pl.BlockSpec(memory_space=pltpu.VMEM) for _ in out_shape),
         scratch_shapes=scratch,
         compiler_params=pltpu.CompilerParams(
-            collective_id=0, has_side_effects=True, vmem_limit_bytes=64 * 1024 * 1024
+            collective_id=0, has_side_effects=True, vmem_limit_bytes=63 * 1024 * 1024
         ),
     )(
         normed, queries, keys_t, values_t, context_grad, segments, w_query, w_key, w_value,
@@ -684,7 +671,7 @@
         in_specs=[pl.BlockSpec(memory_space=pltpu.VMEM)] * 4,
         out_specs=tuple(pl.BlockSpec(memory_space=pl.ANY) for _ in out_shape),
         scratch_shapes=[dma((4,))],
-        compiler_params=pltpu.CompilerParams(vmem_limit_bytes=64 * 1024 * 1024),
+        compiler_params=pltpu.CompilerParams(vmem_limit_bytes=512 * 1024),
     )(*results)
 
 

time: 52.6 us -> 50.6 us (0.962)
  Pallas kernels: 51.8 us -> 49.9 us
    pallas_call x1, Pallas kernels: 50.1 us -> 49.1 us  [per_device(): pl.pallas_call(functools.partial(kernel, ndp), out_shape=tuple((pltpu.VME...]
    pallas_call x1, Pallas kernels: 1.71 us -> 0.75 us  [per_device(): pl.pallas_call(hand_over, out_shape=out_shape, in_specs=[pl.BlockSpec(mem...]
where the time goes in v4:
time: 50.6 us; the launch traced here: 50.5 us
  Pallas kernels  49.9 us (99%)
  between operations  0.65 us (1%)
    pallas_call x1, Pallas kernels, per_device(): pl.pallas_call(functools.partial(kernel, ndp), out_shape=tuple((pltpu.VME...  49.1 us

profile of v4, /device:TPU:1, one launch (start us, length us, event | category | flops | bytes accessed | tf_op | source)
XLA Modules:
  0.0 50.5 jit_solution(3731684361253078724)
XLA Ops:
  0.6 49.1 %shard_map.192 = (bf16[1,256,512]{2,1,0:T(8,128)(2,1)S(1)}, f32[3,2,512]{2,1,0:T(2,128)S(1)}, f32[2,256]{1,0:T(2,128)S(1)}, f32[2,2,16]{2,1,0:T(2,128)S(1)}) custom-call(bf16[1,256,512]{2,1,0:T(8,128)(2,1)} %normed_h.1, bf16[1,256,256]{2,1,0:T(8,128)(2,1)} %queries_h.1, bf16[16,256]{1,0:T(8,128)(2,1)} %bitcast.6, bf16[16,256]{1,0:T(8,128)(2,1)} %bitcast.7, ...), custom_call_target="tpu_custom_call" | custom-call | tf_op jit(solution)/shard_map/pallas_call | solution.py:654
  49.8 0.7 %shard_map.193 = (bf16[1,256,512]{2,1,0:T(8,128)(2,1)}, f32[3,2,512]{2,1,0:T(2,128)}, f32[2,256]{1,0:T(2,128)}, f32[2,2,16]{2,1,0:T(2,128)}) custom-call(bf16[1,256,512]{2,1,0:T(8,128)(2,1)S(1)} %get-tuple-element.8.refs_0_, f32[3,2,512]{2,1,0:T(2,128)S(1)} %get-tuple-element.9.refs_1_, f32[2,256]{1,0:T(2,128)S(1)} %get-tuple-element.10.refs_2_, ...), custom_call_target="tpu_custom_call" | custom-call | tf_op jit(solution)/shard_map/pallas_call | solution.py:668

commit v5 on v4

--- a/solution.py
+++ b/solution.py
@@ -56,33 +56,14 @@
     return lax.dot_general(left, right, (((0,), (0,)), ((), ())), preferred_element_type=F32)
 
 
-CHUNKS = ((0, 128, "z"), (128, 224, "z"), (224, 256, "y"))
+CHUNKS = ((0, 128, 'z'), (128, 224, 'z'), (224, 256, 'y'))
 
 FAR = (
     (2, 2), (2, 1), (2, -1), (1, 2), (-1, 2), (0, 2), (1, 1), (1, -1), (-1, 1), (-1, -1),
     (2, 0), (0, 1), (0, -1), (1, 0), (-1, 0), (0, 0),
 )
 
-ORDER = (
-    ("first", 1), ("first", 2), ("up",), ("fwd", 0, 0), ("w",), ("mm", 0, 0), ("spr", 0, 0, 1),
-    ("spr", 0, 0, -1), ("col", 0, 1), ("col", 0, -1), ("rsy", 1), ("col", 1, 1), ("col", 1, -1),
-    ("rsy", 0), ("spr", 1, 0, 1), ("spr", 1, 0, -1), ("spr", 2, 0, 1), ("spr", 2, 0, -1),
-    ("fwd", 0, 1), ("fwd", 0, -1), ("col", 2, 1), ("col", 2, -1), ("fwd", 1, 0), ("fwd", -1, 0),
-    ("mm", 0, 1), ("mm", 0, -1), ("mm", 1, 0), ("col", 0, 2), ("mm", -1, 0), ("spr", 0, 1, 1),
-    ("spr", 0, 1, -1), ("up2",), ("col", 1, 2), ("spr", 0, -1, 1), ("spr", 0, -1, -1),
-    ("rsz", 1), ("gfirst", 1), ("fwd", 0, 2), ("spr", 1, 1, 1), ("spr", 1, 1, -1),
-    ("spr", 2, 1, 1), ("spr", 2, 1, -1), ("fwd", 1, 1), ("rsz", 0), ("gfirst", 0),
-    ("spr", 1, -1, 1), ("spr", 1, -1, -1), ("spr", 2, -1, 1), ("spr", 2, -1, -1),
-    ("fwd", -1, 1), ("fwd", 1, -1), ("fwd", -1, -1), ("mm", 0, 2), ("col", 2, 2), ("fwd", 2, 0),
-    ("mm", 1, 1), ("mm", -1, 1), ("gcol", 1, 1), ("gcol", 1, -1), ("spr", 0, 2, 1),
-    ("spr", 0, 2, -1), ("mm", 1, -1), ("mm", -1, -1), ("mm", 2, 0), ("gcol", 0, 1),
-    ("gcol", 0, -1), ("gcol", 1, 2), ("spr", 2, 2, 1), ("spr", 2, 2, -1), ("spr", 1, 2, 1),
-    ("spr", 1, 2, -1), ("fwd", 1, 2), ("fwd", -1, 2), ("gcol", 0, 2), ("mm", 1, 2),
-    ("fwd", 2, 1), ("mm", -1, 2), ("dp",), ("gfwd", 1, 0), ("fwd", 2, -1), ("mm", 2, 1),
-    ("gfwd", 0, 0), ("mm", 2, -1), ("gfwd", 1, 1), ("gfwd", 1, -1), ("fwd", 2, 2),
-    ("gfwd", 0, 1), ("gfwd", 0, -1), ("gfwd", 1, 2), ("mm", 2, 2), ("gfwd", 0, 2), ("kv", 1),
-    ("kv", 0), ("dpout",),
-)
+ORDER = (('up',), ('fwd', 0, 0, 0), ('fwd', 1, 0, 0), ('fwd', 2, 0, 0), ('w',), ('mm', 0, 0), ('spr', 0, 0, 1), ('spr', 0, 0, -1), ('fwd', 0, 1, 0), ('fwd', 0, -1, 0), ('col', 0, 1), ('col', 0, -1), ('fwd', 0, 0, 1), ('fwd', 0, 0, -1), ('rsy', 1), ('col', 1, 1), ('col', 1, -1), ('fwd', 1, 0, 1), ('fwd', 1, 0, -1), ('rsy', 0), ('spr', 1, 0, 1), ('spr', 1, 0, -1), ('spr', 2, 0, 1), ('spr', 2, 0, -1), ('fwd', 1, 1, 0), ('fwd', 1, -1, 0), ('fwd', 2, 0, 1), ('fwd', 2, 0, -1), ('col', 2, 1), ('col', 2, -1), ('fwd', 2, 1, 0), ('fwd', 2, -1, 0), ('mm', 0, 1), ('mm', 1, 0), ('mm', -1, 0), ('fwd', 0, 2, 0), ('mm', 0, -1), ('col', 0, 2), ('fwd', 0, 0, 2), ('spr', 0, 1, 1), ('spr', 0, 1, -1), ('fwd', 0, 1, 1), ('fwd', 0, -1, 1), ('up2',), ('col', 1, 2), ('fwd', 1, 0, 2), ('spr', 0, -1, 1), ('spr', 0, -1, -1), ('fwd', 0, 1, -1), ('fwd', 0, -1, -1), ('rsz', 1), ('gfirst', 1), ('fwd', 2, 0, 2), ('spr', 1, 1, 1), ('spr', 1, 1, -1), ('fwd', 1, 1, 1), ('fwd', 1, -1, 1), ('spr', 2, 1, 1), ('spr', 2, 1, -1), ('fwd', 2, 1, 1), ('fwd', 2, 1, -1), ('mm', 0, 2), ('rsz', 0), ('gfirst', 0), ('spr', 1, -1, 1), ('spr', 1, -1, -1), ('spr', 2, -1, 1), ('spr', 2, -1, -1), ('fwd', 2, -1, 1), ('fwd', 1, 1, -1), ('fwd', 1, -1, -1), ('fwd', 1, 2, 0), ('fwd', 2, -1, -1), ('mm', 1, 1), ('col', 2, 2), ('fwd', 2, 2, 0), ('mm', -1, 1), ('mm', 1, -1), ('mm', -1, -1), ('mm', 2, 0), ('gcol', 1, 1), ('spr', 0, 2, 1), ('spr', 0, 2, -1), ('gcol', 1, -1), ('fwd', 0, 1, 2), ('fwd', 0, -1, 2), ('fwd', 2, 1, 2), ('fwd', 0, 2, 1), ('gcol', 0, 1), ('gcol', 0, -1), ('fwd', 2, -1, 2), ('gcol', 1, 2), ('spr', 2, 2, 1), ('spr', 2, 2, -1), ('fwd', 2, 2, 1), ('fwd', 2, 2, -1), ('spr', 1, 2, 1), ('spr', 1, 2, -1), ('fwd', 1, 1, 2), ('fwd', 1, -1, 2), ('gcol', 0, 2), ('fwd', 0, 2, -1), ('mm', 1, 2), ('mm', -1, 2), ('fwd', 1, 2, 1), ('dp',), ('gfwd', 1, 0), ('fwd', 1, 2, -1), ('fwd', 2, 2, 2), ('mm', 2, 1), ('gfwd', 0, 0), ('fwd', 0, 2, 2), ('mm', 2, -1), ('gfwd', 1, 1), ('gfwd', 1, -1), ('fwd', 1, 2, 2), ('gfwd', 0, 1), ('gfwd', 0, -1), ('gfwd', 1, 2), ('mm', 2, 2), ('gfwd', 0, 2), ('kv', 1), ('kv', 0), ('dpout',))
 
 
 def kernel(
@@ -98,14 +79,22 @@
 ):
     i = lax.axis_index("tensor")
     b = lax.axis_index("dp")
-    core = i % 2
-    z = (i // 2) % NZ
+    core = lax.rem(i, 2)
+    z = lax.rem(i // 2, NZ)
     y = i // (2 * NZ)
     side = i // HALF
     own_in = core == side
 
+    rows_at = [lax.rem(y + d, NY) * (2 * NZ) for d in range(NY)]
+    cols_at = [lax.rem(z + d, NZ) * 2 for d in range(NZ)]
+    chip_at = [[r + c for c in cols_at] for r in rows_at]
+    cores = (core, 1 - core)
+
     def dev(dy, dz, dc):
-        return (((y + dy) % NY) * NZ + (z + dz) % NZ) * 2 + (core + dc) % 2
+        return chip_at[dy % NY][dz % NZ] + cores[dc]
+
+    def dev_side(dy, dz):
+        return chip_at[dy % NY][dz % NZ] + side
 
     loads = [
         (keys_h, kvown.at[0]), (values_h, kvown.at[1]), (queries_h.at[0], queries),
@@ -200,7 +189,7 @@
 
     def scatter_home(src, dst, send, recv, lanes=slice(None)):
         for dy, dz in FAR:
-            to = dev(dy, dz, side - core)
+            to = dev_side(dy, dz)
 
             def start():
                 remote(
@@ -220,7 +209,7 @@
 
     def along_z(src, dst, n, lanes):
         for dz in (2, 1, -1, 0):
-            to = dev(0, dz, side - core)
+            to = dev_side(0, dz)
 
             def start():
                 remote(
@@ -245,10 +234,10 @@
                 remote(ref, ref, ys.at[n], yr.at[n], (b, dev(dy, 0, 0))).start()
 
     early, late = slice(0, T // 2), slice(T // 2, T)
-    along_z(kvown.at[1], vt, 0, late)
     scatter_home(kvown.at[0], kt, kvs.at[0], kvr.at[0], early)
     scatter_home(kvown.at[1], vt, kvs.at[1], kvr.at[1], early)
     scatter_home(kvown.at[0], kt, kvs.at[2], kvr.at[2], late)
+    scatter_home(kvown.at[1], vt, kvs.at[3], kvr.at[3], late)
     loads[8].wait()
     rank = lax.broadcasted_iota(jnp.int32, (RANK, 128), 0)
     lane = lax.broadcasted_iota(jnp.int32, (RANK, 128), 1)
@@ -369,7 +358,6 @@
 
     every = slice(0, T)
     wait_home(0, kt, early)
-    along_y(vt, 0, late)
     probs_early = [softmax(h, early, early) for h in heads]
     wait_home(1, vt, early)
     grads_early = []
@@ -386,18 +374,20 @@
             cot[:, h], probs_early[n].astype(BF16), probs[n].astype(BF16)
         ).astype(BF16)
         send_rsy(1, n)
-    by(own_in, yr.at[0], vt.at[0:HD, late], vt.at[:, late])
+    wait_home(3, vt, late)
     grads = []
     for n, h in enumerate(heads):
         grads.append(score_cotangent(h, late, every, probs[n]))
+        query_cotangent(h, late, every, grads[n])
+    for n in range(1, len(CHUNKS)):
+        gathers[n].first()
+    for n, h in enumerate(heads):
         key_rot = both(queries[:, h], grads_early[n], grads[n]) * scale
         one, two = key_rot[: HD // 2], key_rot[HD // 2 :]
         rs_src[0, n] = jnp.concatenate(
             [one * cosine + two * sine, two * cosine - one * sine], axis=0
         ).astype(BF16)
         send_rsy(0, n)
-    for n, h in enumerate(heads):
-        query_cotangent(h, late, every, grads[n])
     lax.fori_loop(0, NT, load_w, 0)
 
     def step_first(tag):
@@ -409,11 +399,11 @@
     def step_spr(tag, d, e):
         gathers[tag].spr(d, e)
 
-    def step_fwd(dy, dz):
+    def step_fwd(n, dy, dz):
+        gathers[n].far(dy, dz)
         slot = dev(dy, dz, 0)
-        for n in range(len(CHUNKS)):
-            gathers[n].far(dy, dz)
-        remote(qall.at[slot], qall.at[slot], fs, fr.at[slot], (b, other)).start()
+        ref = gathers[n].ref(slot, None)
+        remote(ref, ref, fs, fr.at[slot], (b, other)).start()
 
     def push_g(p, slot, to):
         ref = g_ref(p, slot)
@@ -555,10 +545,9 @@
         steps[name](*rest)
     out_i[0] = acc[...].astype(BF16)
 
-    for n in range(3):
+    for n in range(4):
         by(own_in, kvs.at[n], kt.at[0:240, early], kt.at[:, early])
-    for n, lanes in enumerate((late, slice(None))):
-        ref = (vt, ut)[n]
+    for n, lanes, ref in ((1, slice(None), ut),):
         by(own_in, zs.at[n], ref.at[0:48, lanes], ref.at[0:64, lanes])
 
         @pl.when(own_in)
@@ -640,7 +629,7 @@
         vmem((T, NC), F32),
         vmem((T, T), F32),
         dma((16,)), dma,
-        dma((3,)), dma((3,)), dma((2,)), dma((2,)), dma((2,)), dma((2,)),
+        dma((4,)), dma((4,)), dma((2,)), dma((2,)), dma((2,)), dma((2,)),
         dma((2,)), dma((2,)), dma((2,)), dma((2,)),
         dma((len(CHUNKS),)), dma((len(CHUNKS), NT)), dma, dma((NT,)), dma((4,)), dma((2, NT)),
         dma, dma, dma, dma, dma, dma,

time: 50.6 us -> 50.6 us (level)
  no operation moved by 1% of the time
where the time goes in v5:
time: 50.6 us; the launch traced here: 50.5 us
  Pallas kernels  49.8 us (98%)
  between operations  0.65 us (1%)
    pallas_call x1, Pallas kernels, per_device(): pl.pallas_call(functools.partial(kernel, ndp), out_shape=tuple((pltpu.VME...  49.1 us

profile of v5, /device:TPU:1, one launch (start us, length us, event | category | flops | bytes accessed | tf_op | source)
XLA Modules:
  0.0 50.5 jit_solution(8340302261343586363)
XLA Ops:
  0.6 49.1 %shard_map.192 = (bf16[1,256,512]{2,1,0:T(8,128)(2,1)S(1)}, f32[3,2,512]{2,1,0:T(2,128)S(1)}, f32[2,256]{1,0:T(2,128)S(1)}, f32[2,2,16]{2,1,0:T(2,128)S(1)}) custom-call(bf16[1,256,512]{2,1,0:T(8,128)(2,1)} %normed_h.1, bf16[1,256,256]{2,1,0:T(8,128)(2,1)} %queries_h.1, bf16[16,256]{1,0:T(8,128)(2,1)} %bitcast.6, bf16[16,256]{1,0:T(8,128)(2,1)} %bitcast.7, ...), custom_call_target="tpu_custom_call" | custom-call | tf_op jit(solution)/shard_map/pallas_call | solution.py:643
  49.7 0.7 %shard_map.193 = (bf16[1,256,512]{2,1,0:T(8,128)(2,1)}, f32[3,2,512]{2,1,0:T(2,128)}, f32[2,256]{1,0:T(2,128)}, f32[2,2,16]{2,1,0:T(2,128)}) custom-call(bf16[1,256,512]{2,1,0:T(8,128)(2,1)S(1)} %get-tuple-element.8.refs_0_, f32[3,2,512]{2,1,0:T(2,128)S(1)} %get-tuple-element.9.refs_1_, f32[2,256]{1,0:T(2,128)S(1)} %get-tuple-element.10.refs_2_, ...), custom_call_target="tpu_custom_call" | custom-call | tf_op jit(solution)/shard_map/pallas_call | solution.py:657
